TPU v7x, 512 devices: a whole 4x4x16 slice. The times are simulated.
512 devices in a mesh: branch: 128 (over x, z, core), sub: 4 (over y).
Axes of the slice: x: 4, y: 4, z: 16, core: 2. Of those that a mesh axis runs over, the one named last changes fastest.
Arguments:
- rhs: bfloat16 [16, 2097152], P(None, ('branch', 'sub')), may hold values from -6 to 6
- coords: bfloat16 [3, 2097152], P(None, ('branch', 'sub')), may hold values from 0 to 1, as said below
- basis: bfloat16 [8192, 64, 256], P(('branch', 'sub')), may hold values from -0.375 to 0.375
- leaf_transfer: bfloat16 [8192, 64, 64], P(('branch', 'sub')), may hold values from -0.1875 to 0.1875
- device_transfer: bfloat16 [512, 64, 64], P(('branch', 'sub')), may hold values from -0.375 to 0.375
- transfer_one: bfloat16 [128, 64, 64], replicated, may hold values from -0.5 to 0.5
- transfer_two: bfloat16 [64, 64, 64], replicated, may hold values from -0.5 to 0.5
- transfer_three: bfloat16 [32, 64, 64], replicated, may hold values from -0.5 to 0.5
- far_list: int32 [512, 16], P(('branch', 'sub')), may hold values from 0 to 511, as said below
- far_count: int32 [512], P(('branch', 'sub')), may hold values from 1 to 16, as said below
- far_coupling: bfloat16 [512, 16, 64, 64], P(('branch', 'sub')), may hold values from -1.796875 to 1.796875
- top_list: int32 [128, 4, 8], P('branch'), may hold values from 0 to 127, as said below
- top_coupling: bfloat16 [128, 4, 8, 64, 64], P('branch'), may hold values from -1.796875 to 1.796875
- near_list: int32 [8192, 8], P(('branch', 'sub')), may hold values from 0 to 8191, as said below
Outputs:
- result: float32 [16, 2097152], P(None, ('branch', 'sub'))
Inputs may be any that keep to these rules, and one draw needn't show every extreme that they name: `coords`: each leaf's points lie in and around that leaf's own cell of a grid of 8192 cells in the unit cube; consecutive leaves have nearby cells. `near_list`: row i starts with i itself; the other entries are distinct leaves of the cluster i // 16 or of the clusters just before and after it in the order branch, then sub. `far_list`: the entries of a row are distinct and differ from the row's own cluster; only the first far_count slots are read. `far_count`: some cluster uses all 16 slots. `top_list`: entry [b, l, j] names a node of level l + 1, so it is below 128 // 2**l.
All inputs are finite; a program needn't handle non-finite values.
Results may differ from a plain program's by a relative error of at most 0.0029.
Values may be sent and summed in bfloat16 or wider, within the bound.
No kernel may reach another device: no remote copies, remote signals or barrier semaphores. Data moves between devices by JAX's collectives and lax.ppermute only.
A program may use at most 64 MiB of HBM per device.

v0:
```python
import jax
import jax.numpy as jnp
from jax import lax
from jax.sharding import PartitionSpec as P

INV_LENGTH = 20.0
PRECISE = lax.Precision.HIGHEST


def swapped(value, axis, distance):
    mask = 2**distance
    pairs = [(source, source ^ mask) for source in range(lax.axis_size(axis))]
    return lax.ppermute(value, axis, pairs)


def shifted(value, axis, by):
    size = lax.axis_size(axis)
    pairs = [(i, i + by) for i in range(size) if 0 <= i + by < size]
    return lax.ppermute(value, axis, pairs)


def kernel_tile(target_xyz, source_xyz):
    spread_xyz = target_xyz[:, None, :, None] - source_xyz[:, :, None, :]
    squared = jnp.sum(spread_xyz * spread_xyz, axis=0)
    return jnp.exp(-INV_LENGTH * jnp.sqrt(squared)).astype(jnp.bfloat16)


def pair_up(child, transfer):
    raised = jnp.einsum("nij,njr->nir", transfer.astype(jnp.float32), child, precision=PRECISE)
    return jnp.sum(raised.reshape(-1, 2, raised.shape[1], raised.shape[2]), axis=1)


def lower(parent, transfer_row):
    return jnp.einsum("ij,ir->jr", transfer_row.astype(jnp.float32), parent, precision=PRECISE)


def on_device(
    rhs,
    coords,
    basis,
    leaf_transfer,
    device_transfer,
    transfer_one,
    transfer_two,
    transfer_three,
    far_list,
    far_count,
    far_coupling,
    top_list,
    top_coupling,
    near_list,
):
    n_sub = lax.axis_size("sub")
    branch_id = lax.axis_index("branch")
    device_id = branch_id * n_sub + lax.axis_index("sub")
    leaves_here, rank_dim, leaf_size = basis.shape
    columns = rhs.shape[0]
    rhs_blocks = rhs.reshape(columns, leaves_here, leaf_size)
    leaf_coeffs = jnp.einsum("lkp,rlp->lkr", basis, rhs_blocks, preferred_element_type=jnp.float32)
    coarse = jnp.einsum(
        "lij,ljr->ir", leaf_transfer.astype(jnp.float32), leaf_coeffs, precision=PRECISE
    )
    lifted = jnp.dot(device_transfer[0].astype(jnp.float32), coarse, precision=PRECISE)
    all_coarse = lax.all_gather(coarse[None], ("branch", "sub"), axis=0, tiled=True)
    level_one = lax.psum(lifted, "sub")
    all_one = lax.all_gather(level_one[None], "branch", axis=0, tiled=True)
    all_two = pair_up(all_one, transfer_one)
    all_three = pair_up(all_two, transfer_two)
    all_four = pair_up(all_three, transfer_three)
    far_sources = all_coarse[far_list[0]]
    far_terms = jnp.einsum(
        "jik,jkr->jir", far_coupling[0].astype(jnp.float32), far_sources, precision=PRECISE
    )
    live_mask = (jnp.arange(far_terms.shape[0]) < far_count[0]).astype(jnp.float32)
    device_far = jnp.sum(far_terms * live_mask[:, None, None], axis=0)
    levels = (all_one, all_two, all_three, all_four)
    partials = [
        jnp.einsum(
            "jik,jkr->ir",
            top_coupling[0, level].astype(jnp.float32),
            levels[level][top_list[0, level]],
            precision=PRECISE,
        )
        for level in range(4)
    ]
    upper_parts = jnp.stack(partials[1:])
    for bit_index in range(3):
        partner = swapped(upper_parts[bit_index:], "branch", bit_index)
        upper_parts = jnp.concatenate(
            [upper_parts[:bit_index], upper_parts[bit_index:] + partner], axis=0
        )
    down_four = upper_parts[2]
    down_three = upper_parts[1] + lower(down_four, transfer_three[branch_id // 4])
    down_two = upper_parts[0] + lower(down_three, transfer_two[branch_id // 2])
    down_one = partials[0] + lower(down_two, transfer_one[branch_id])
    down_zero = device_far + lower(down_one, device_transfer[0])
    leaf_down = jnp.einsum(
        "lij,ir->ljr", leaf_transfer.astype(jnp.float32), down_zero, precision=PRECISE
    ).astype(jnp.bfloat16)
    far_part = jnp.einsum("lkp,lkr->lrp", basis, leaf_down, preferred_element_type=jnp.float32)

    def neighbour(shift_by):
        return shifted((rhs, coords), ("branch", "sub"), shift_by)

    before = neighbour(1)
    after = neighbour(-1)
    wide_rhs = jnp.concatenate([before[0], rhs, after[0]], axis=1).reshape(
        columns, 3 * leaves_here, leaf_size
    )
    wide_xyz = jnp.concatenate([before[1], coords, after[1]], axis=1).reshape(
        3, 3 * leaves_here, leaf_size
    )
    local_sources = near_list - (device_id - 1) * leaves_here
    target_xyz = jnp.transpose(coords.reshape(3, leaves_here, leaf_size), (1, 0, 2))

    def near_leaf(operands):
        sources, target_here = operands
        tile_vals = kernel_tile(
            target_here.astype(jnp.float32), wide_xyz[:, sources].astype(jnp.float32)
        )
        return jnp.einsum(
            "rjq,jpq->rp", wide_rhs[:, sources], tile_vals, preferred_element_type=jnp.float32
        )

    near_part = lax.map(near_leaf, (local_sources, target_xyz))
    total = near_part + far_part
    return jnp.transpose(total, (1, 0, 2)).reshape(columns, leaves_here * leaf_size)


def solution(mesh):
    in_specs = (
        P(None, ("branch", "sub")),
        P(None, ("branch", "sub")),
        P(("branch", "sub"), None, None),
        P(("branch", "sub"), None, None),
        P(("branch", "sub"), None, None),
        P(),
        P(),
        P(),
        P(("branch", "sub"), None),
        P(("branch", "sub")),
        P(("branch", "sub"), None, None, None),
        P("branch", None, None),
        P("branch", None, None, None, None),
        P(("branch", "sub"), None),
    )
    out_specs = P(None, ("branch", "sub"))
    return jax.shard_map(
        on_device, mesh=mesh, in_specs=in_specs, out_specs=out_specs, check_vma=False
    )
```

profile of v0, /device:TPU:1, one launch (start us, length us, event | category | flops | bytes accessed | tf_op | source)
XLA Modules:
  0.0 382.2 jit_solution(2599500705626678968)
XLA Ops:
  6.5 4.2 %collective-permute-start = (bf16[16,4096]{1,0:T(8,128)(2,1)}, bf16[16,4096]{1,0:T(8,128)(2,1)}, u32[]{:S(2)}, u32[]{:S(2)}) collective-permute-start(bf16[16,4096]{1,0:T(8,128)(2,1)} %param.16), channel_id=1, source_target_pairs={{0,1},{1,2},{2,3},{3,4},{4,5},{5,6},{6,7},{7,8},{8,9},{9,10},{10,1... | collective-permute-start | bytes 393224 | tf_op jit(solution)/shard_map/ppermute | solution.py:19
  10.7 3.9 %collective-permute-start.1 = (bf16[16,4096]{1,0:T(8,128)(2,1)}, bf16[16,4096]{1,0:T(8,128)(2,1)}, u32[]{:S(2)}, u32[]{:S(2)}) collective-permute-start(bf16[16,4096]{1,0:T(8,128)(2,1)} %param.16), channel_id=1, source_target_pairs={{1,0},{2,1},{3,2},{4,3},{5,4},{6,5},{7,6},{8,7},{9,8},{10,9},{11,1... | collective-permute-start | bytes 393224 | tf_op jit(solution)/shard_map/ppermute | solution.py:19
  14.6 1.9 collective-permute-start.2
  16.6 4.9 %collective-permute-start.3 = (bf16[3,4096]{1,0:T(4,128)(2,1)}, bf16[3,4096]{1,0:T(4,128)(2,1)}, u32[]{:S(2)}, u32[]{:S(2)}) collective-permute-start(bf16[3,4096]{1,0:T(4,128)(2,1)} %param.17), channel_id=1, source_target_pairs={{1,0},{2,1},{3,2},{4,3},{5,4},{6,5},{7,6},{8,7},{9,8},{10,9},{11,1... | collective-permute-start | bytes 73736 | tf_op jit(solution)/shard_map/ppermute | solution.py:19
  25.7 8.3 %psum.7 = f32[1,64,16]{1,2,0:T(8,128)S(1)} all-reduce(f32[1,64,16]{1,2,0:T(8,128)S(1)} %convolution_bitcast_fusion.5), channel_id=1, replica_groups=mesh['branch'=128,'sub'=4] {'sub'}, use_global_device_ids=true, to_apply=%region_4.0 | all-reduce | flops 1024 | bytes 8192 | tf_op jit(solution)/shard_map/psum | solution.py:65
  34.0 120.1 %all_gather.7 = f32[128,64,16]{1,2,0:T(8,128)} all-gather(f32[1,64,16]{1,2,0:T(8,128)S(1)} %psum.7), channel_id=1, replica_groups=mesh['branch'=128,'sub'=4] {'branch'}, dimensions={0}, use_global_device_ids=true | all-gather | bytes 528384 | tf_op jit(solution)/shard_map/all_gather | solution.py:66
  154.1 3.9 %copy.41 = bf16[128,64,64]{2,1,0:T(8,128)(2,1)S(1)} copy(bf16[128,64,64]{0,2,1:T(8,128)(2,1)} %param.21) | data formatting | bytes 2097152 | tf_op args[5]
  158.1 5.4 %bitcast_reduce_fusion = f32[64,64,16]{1,2,0:T(8,128)} fusion(f32[128,64,16]{1,2,0:T(8,128)} %all_gather.7, bf16[128,64,64]{2,1,0:T(8,128)(2,1)S(1)} %copy.41), kind=kOutput, calls=%fused_computation.34 | convolution fusion | flops 100728832 | bytes 1835008 | tf_op jit(solution)/shard_map/nij,njr->nir/dot_general | solution.py:29
  163.5 1.6 gather_fusion.4
  165.2 2.8 bitcast_reduce_fusion.1
  169.1 1.6 bitcast_reduce_fusion.2
  175.1 2.1 collective-permute-start.4
  177.2 1.8 gather_fusion.3
  180.2 1.9 collective-permute-start.5
  182.8 1.9 collective-permute-done.5
  184.7 2.6 collective-permute-start.6
  187.4 2.6 collective-permute-done.6
  191.0 1.5 pad_maximum_fusion.1
  194.5 83.8 %while.10 = (s32[]{:T(128)}, f32[16,16,256]{2,1,0:T(8,128)}, s32[16,8]{1,0:T(8,128)S(1)}, bf16[16,48,256]{2,0,1:T(8,128)(2,1)}, bf16[16,3,256]{2,1,0:T(4,128)(2,1)S(1)}, /*index=5*/bf16[3,48,256]{2,0,1:T(4,128)(2,1)}, s32[]{:T(128)}) while((s32[]{:T(128)}, f32[16,16,256]{2,1,0:T(8,128)}, s32[16,8]{1,0:T(8,128)S(1)}, ...), condition=%wide.region_2.0_spmd, body=%wide.region_0.2_spmd.sunk | while | flops 22028056 | bytes 4554997 | solution.py:125
  194.5 1.5 gather_fusion
  196.7 1.5 gather_fusion.1
  198.3 1.5 fusion.73
  199.8 1.5 gather_fusion
  202.0 1.5 gather_fusion.1
  203.5 1.5 fusion.73
  205.0 1.5 gather_fusion
  207.2 1.5 gather_fusion.1
  208.7 1.5 fusion.73
  210.2 1.5 gather_fusion
  212.4 1.5 gather_fusion.1
  214.0 1.5 fusion.73
  215.5 1.5 gather_fusion
  217.7 1.5 gather_fusion.1
  219.2 1.5 fusion.73
  220.7 1.5 gather_fusion
  222.9 1.5 gather_fusion.1
  224.4 1.5 fusion.73
  225.9 1.5 gather_fusion
  228.1 1.5 gather_fusion.1
  229.7 1.5 fusion.73
  231.2 1.5 gather_fusion
  233.4 1.5 gather_fusion.1
  234.9 1.5 fusion.73
  236.4 1.5 gather_fusion
  238.6 1.5 gather_fusion.1
  240.1 1.5 fusion.73
  243.8 1.5 gather_fusion.1
  245.4 1.5 fusion.73
  246.9 1.5 gather_fusion
  249.1 1.6 gather_fusion.1
  250.6 1.5 fusion.73
  254.3 1.5 gather_fusion.1
  255.9 1.5 fusion.73
  257.4 1.5 gather_fusion
  259.5 1.5 gather_fusion.1
  261.1 1.5 fusion.73
  264.8 1.5 gather_fusion.1
  266.3 1.5 fusion.73
  270.0 1.5 gather_fusion.1
  271.6 1.5 fusion.73
  275.2 1.5 gather_fusion.1
  276.8 1.5 fusion.73
  278.3 90.6 %all-gather.4.cloned.1.call-done = f32[512,64,16]{1,2,0:T(8,128)} async-done(((f32[1,64,16]{1,2,0:T(8,128)}), f32[512,64,16]{1,2,0:T(8,128)}) %all-gather.4.cloned.1.call-update) | async-done | bytes 2097168 | tf_op jit(solution)/shard_map/all_gather | solution.py:64
  368.8 2.7 gather_fusion.2
  (160 shorter events, 36.2 us)
Async XLA Ops:
  6.5 158.6 %copy-start = (bf16[64,64,64]{2,1,0:T(8,128)(2,1)S(1)}, bf16[64,64,64]{2,1,0:T(8,128)(2,1)}, u32[]{:S(2)}) copy-start(bf16[64,64,64]{2,1,0:T(8,128)(2,1)} %param.22) | copy-start | bytes 1572868
  6.5 362.3 %all-gather.4.cloned.1.call-start = ((), (), s32[]{:S(2)}) async-start(), calls=%async_computation | async-start | bytes 4202496 | tf_op jit(solution)/shard_map/all_gather | solution.py:64
  6.5 186.1 %collective-permute-start = (bf16[16,4096]{1,0:T(8,128)(2,1)}, bf16[16,4096]{1,0:T(8,128)(2,1)}, u32[]{:S(2)}, u32[]{:S(2)}) collective-permute-start(bf16[16,4096]{1,0:T(8,128)(2,1)} %param.16), channel_id=1, source_target_pairs={{0,1},{1,2},{2,3},{3,4},{4,5},{5,6},{6,7},{7,8},{8,9},{9,10},{10,1... | collective-permute-start | bytes 393224 | tf_op jit(solution)/shard_map/ppermute | solution.py:19
  10.7 181.9 %collective-permute-start.1 = (bf16[16,4096]{1,0:T(8,128)(2,1)}, bf16[16,4096]{1,0:T(8,128)(2,1)}, u32[]{:S(2)}, u32[]{:S(2)}) collective-permute-start(bf16[16,4096]{1,0:T(8,128)(2,1)} %param.16), channel_id=1, source_target_pairs={{1,0},{2,1},{3,2},{4,3},{5,4},{6,5},{7,6},{8,7},{9,8},{10,9},{11,1... | collective-permute-start | bytes 393224 | tf_op jit(solution)/shard_map/ppermute | solution.py:19
  14.6 176.3 %collective-permute-start.2 = (bf16[3,4096]{1,0:T(4,128)(2,1)}, bf16[3,4096]{1,0:T(4,128)(2,1)}, u32[]{:S(2)}, u32[]{:S(2)}) collective-permute-start(bf16[3,4096]{1,0:T(4,128)(2,1)} %param.17), channel_id=1, source_target_pairs={{0,1},{1,2},{2,3},{3,4},{4,5},{5,6},{6,7},{7,8},{8,9},{9,10},{10,1... | collective-permute-start | bytes 73736 | tf_op jit(solution)/shard_map/ppermute | solution.py:19
  16.6 174.4 %collective-permute-start.3 = (bf16[3,4096]{1,0:T(4,128)(2,1)}, bf16[3,4096]{1,0:T(4,128)(2,1)}, u32[]{:S(2)}, u32[]{:S(2)}) collective-permute-start(bf16[3,4096]{1,0:T(4,128)(2,1)} %param.17), channel_id=1, source_target_pairs={{1,0},{2,1},{3,2},{4,3},{5,4},{6,5},{7,6},{8,7},{9,8},{10,9},{11,1... | collective-permute-start | bytes 73736 | tf_op jit(solution)/shard_map/ppermute | solution.py:19
  24.8 133.3 %copy-start.4 = (f32[16,64,1]{1,0,2:T(8,128)}, f32[16,64,1]{1,0,2:T(8,128)S(1)}, u32[]{:S(2)}) copy-start(f32[16,64,1]{1,0,2:T(8,128)S(1)} %fusion.48) | copy-start | bytes 12292
  165.1 4.0 %copy-start.3 = (bf16[32,64,64]{2,1,0:T(8,128)(2,1)S(1)}, bf16[32,64,64]{2,1,0:T(8,128)(2,1)}, u32[]{:S(2)}) copy-start(bf16[32,64,64]{2,1,0:T(8,128)(2,1)} %param.23) | copy-start | bytes 786436
  165.1 13.8 %copy-start.8 = (s32[1,16]{1,0:T(1,128)S(1)}, s32[1,16]{1,0:T(1,128)}, u32[]{:S(2)}) copy-start(s32[1,16]{1,0:T(1,128)} %param.24) | copy-start | bytes 196
  165.2 13.8 %copy-start.7 = (s32[16,8]{0,1:T(8,128)S(1)}, s32[16,8]{0,1:T(8,128)}, u32[]{:S(2)}) copy-start(s32[16,8]{0,1:T(8,128)} %param.29) | copy-start | bytes 1540
  168.0 23.0 %copy-start.6 = (bf16[3,4096]{1,0:T(4,128)(2,1)S(1)}, bf16[3,4096]{1,0:T(4,128)(2,1)}, u32[]{:S(2)}) copy-start(bf16[3,4096]{1,0:T(4,128)(2,1)} %param.17) | copy-start | bytes 73732
  175.1 5.1 %collective-permute-start.4 = (f32[3,64,16]{1,2,0:T(8,128)S(1)}, f32[3,64,16]{1,2,0:T(8,128)S(1)}, u32[]{:S(2)}, u32[]{:S(2)}) collective-permute-start(f32[3,64,16]{1,2,0:T(8,128)S(1)} %pad_maximum_fusion.2), channel_id=1, source_target_pairs={{0,4},{4,0},{8,12},{12,8},{16,20},{20,16},{24,28},{28,24},{32,36},... | collective-permute-start | bytes 36872 | tf_op jit(solution)/shard_map/ppermute | solution.py:13
  180.2 4.5 %collective-permute-start.5 = (f32[2,64,16]{1,2,0:T(8,128)S(1)}, f32[2,64,16]{1,2,0:T(8,128)S(1)}, u32[]{:S(2)}, u32[]{:S(2)}) collective-permute-start(f32[2,64,16]{1,2,0:T(8,128)S(1)} %slice.70), channel_id=1, source_target_pairs={{0,8},{4,12},{8,0},{12,4},{16,24},{20,28},{24,16},{28,20},{32,40},... | collective-permute-start | bytes 24584 | tf_op jit(solution)/shard_map/ppermute | solution.py:13
  184.7 5.3 %collective-permute-start.6 = (f32[1,64,16]{1,2,0:T(8,128)S(1)}, f32[1,64,16]{1,2,0:T(8,128)S(1)}, u32[]{:S(2)}, u32[]{:S(2)}) collective-permute-start(f32[1,64,16]{1,2,0:T(8,128)S(1)} %slice.72), channel_id=1, source_target_pairs={{0,16},{4,20},{8,24},{12,28},{16,0},{20,4},{24,8},{28,12},{32,48},... | collective-permute-start | bytes 12296 | tf_op jit(solution)/shard_map/ppermute | solution.py:13
  194.5 178.6 %copy-start.5 = (bf16[1,64,64]{2,1,0:T(8,128)(2,1)S(1)}, bf16[1,64,64]{2,1,0:T(8,128)(2,1)}, u32[]{:S(2)}) copy-start(bf16[1,64,64]{2,1,0:T(8,128)(2,1)} %param.20) | copy-start | bytes 24580
  194.5 178.7 %copy-start.2 = (bf16[16,64,64]{2,1,0:T(8,128)(2,1)S(1)}, bf16[16,64,64]{2,1,0:T(8,128)(2,1)}, u32[]{:S(2)}) copy-start(bf16[16,64,64]{2,1,0:T(8,128)(2,1)} %param.19) | copy-start | bytes 393220
  278.3 95.2 %copy-start.1 = (bf16[16,64,256]{2,1,0:T(8,128)(2,1)S(1)}, bf16[16,64,256]{2,1,0:T(8,128)(2,1)}, u32[]{:S(2)}) copy-start(bf16[16,64,256]{2,1,0:T(8,128)(2,1)} %param.18) | copy-start | bytes 1572868
Sparse Core Ops, SparseCore 0:
  177.3 191.5 all-gather.3
where the time goes:
time: 384 us; the launch traced here: 382 us
  blocking collectives  128 us (33%)
  waiting for transfers between devices  95.1 us (25%)
  local copies, waits for them, and re-layouts  62.1 us (16%)
  matrix products  45.3 us (12%)
  starting transfers between devices  21.5 us (6%)
  other arithmetic  14.7 us (4%)
  between operations  14.4 us (4%)
    all_gather x1, blocking collectives, on_device(): all_one = lax.all_gather(level_one[None], 'branch', axis=0, tiled=True)  120 us
    all_gather x1, waiting for transfers between devices, on_device(): lax.all_gather(coarse[None], ('branch', 'sub'), axis=0, tiled=True)  90.6 us
    gather x16, local copies, waits for them, and re-layouts, near_leaf(): wide_rhs[:, sources]  24.7 us
    dot_general x16, matrix products, near_leaf(): jnp.einsum('rjq,jpq->rp', wide_rhs[:, sources], tile_vals, preferred_elem...  23.7 us
    gather x16, local copies, waits for them, and re-layouts, near_leaf(): wide_xyz[:, sources].astype(jnp.float32)  23.6 us
    ppermute x4, starting transfers between devices, shifted(): return lax.ppermute(value, axis, pairs)  14.9 us
    reduce_sum x16, other arithmetic, kernel_tile(): squared = jnp.sum(spread_xyz * spread_xyz, axis=0)  10.6 us
    dot_general x3, matrix products, pair_up(): jnp.einsum('nij,njr->nir', transfer.astype(jnp.float32), child, precision...  9.9 us
  transfers between devices with their start and end apart: 8, of which 3 were waited for; matrix products, arithmetic and copies ran while one was open for 30% of the time, Pallas kernels for 0%

commit v1 on v0

v1 whole, which is shorter than its diff:
```python
import functools

import jax
import jax.numpy as jnp
import numpy as np
from jax import lax
from jax.experimental import pallas as pl
from jax.experimental.pallas import tpu as pltpu
from jax.sharding import Mesh, PartitionSpec as P

F32 = jnp.float32
BF16 = jnp.bfloat16
DEV = ("x", "zh", "zl", "core", "y")
SCALE = float(20.0 * np.log2(np.e))
NT = (((1,), (1,)), ((), ()))
NN = (((1,), (0,)), ((), ()))
GRANT = 60 * 1024 * 1024
PACKED = 10240
ROOM = 98304


def dot(a, b, dims):
    return lax.dot_general(a, b, dims, preferred_element_type=F32)


def split(v):
    hi = v.astype(BF16)
    lo = (v - hi.astype(F32)).astype(BF16)
    return hi, lo


def wide_dot(v, b, dims):
    rows = v.shape[0]
    hi, lo = split(v)
    out = dot(jnp.concatenate([hi, lo], axis=0), b, dims)
    return out[:rows] + out[rows:]


def vmem(n):
    return [pl.BlockSpec(memory_space=pltpu.VMEM)] * n


def hbm(n):
    return [pl.BlockSpec(memory_space=pltpu.HBM)] * n


def smem(n):
    return [pl.BlockSpec(memory_space=pltpu.SMEM)] * n


def copies(sources, targets, sems):
    return [
        pltpu.make_async_copy(source, target, sems.at[k])
        for k, (source, target) in enumerate(zip(sources, targets))
    ]


def up_kernel(
    id_ref, rhs_hbm, coords_hbm, basis_hbm, lt_hbm, dt_hbm,
    out_ref, own_ref, rhs_ref, coords_ref, basis_ref, lt_ref, dt_ref, sems,
):
    moves = copies(
        (rhs_hbm, coords_hbm, basis_hbm, lt_hbm, dt_hbm),
        (rhs_ref, coords_ref, basis_ref, lt_ref, dt_ref),
        sems,
    )
    for move in moves:
        move.start()
    for move in moves:
        move.wait()
    total = jnp.zeros((16, 64), F32)
    for leaf in range(16):
        coeffs = dot(rhs_ref[:, leaf * 256 : (leaf + 1) * 256], basis_ref[leaf], NT)
        total = total + wide_dot(coeffs, lt_ref[leaf], NT)
    lifted = wide_dot(total, dt_ref[0], NT)
    even = (id_ref[0] >> 2) & 1 == 0
    first = jnp.where(even, lifted, total)
    second = jnp.where(even, total, lifted)
    both = jnp.concatenate([first, second], axis=1).astype(BF16)
    for k in range(16):
        out_ref[k] = both
    own_ref[0:16, :] = rhs_ref[...]
    xyz = coords_ref[...].astype(F32)
    own_ref[16:24, :] = jnp.concatenate([xyz, jnp.zeros((5, 4096), F32)], axis=0).astype(BF16)


def up_pass(dev, rhs, coords, basis, lt, dt):
    return pl.pallas_call(
        up_kernel,
        out_shape=[
            jax.ShapeDtypeStruct((16, 16, 128), BF16),
            jax.ShapeDtypeStruct((24, 4096), BF16),
        ],
        in_specs=smem(1) + hbm(5),
        out_specs=vmem(2),
        scratch_shapes=[
            pltpu.VMEM((16, 4096), BF16),
            pltpu.VMEM((3, 4096), BF16),
            pltpu.VMEM((16, 64, 256), BF16),
            pltpu.VMEM((16, 64, 64), BF16),
            pltpu.VMEM((1, 64, 64), BF16),
            pltpu.SemaphoreType.DMA((5,)),
        ],
        compiler_params=pltpu.CompilerParams(vmem_limit_bytes=GRANT),
        cost_estimate=pl.CostEstimate(flops=20_000_000, bytes_accessed=1_000_000, transcendentals=0),
        name="up_pass",
    )(dev, rhs, coords, basis, lt, dt)


def prepare(
    id_ref, t1_ref, t2_ref, t3_ref, fc_ref, tc_ref, packed_ref, path_ref
):
    def put(at, first, second):
        packed_ref[at * 64 : (at + 1) * 64, :] = jnp.concatenate([first, second], axis=1)

    for source, offset, nodes in ((t1_ref, 0, 64), (t2_ref, 64, 32), (t3_ref, 96, 16)):
        for n in range(nodes):
            put(offset + n, source[2 * n], source[2 * n + 1])
    for slot in range(16):
        put(112 + slot, fc_ref[0, slot], fc_ref[0, slot])
    for level in range(4):
        for slot in range(8):
            put(128 + level * 8 + slot, tc_ref[0, level, slot], tc_ref[0, level, slot])
    branch = id_ref[0] >> 2
    path_ref[0] = t1_ref[branch]
    path_ref[1] = t2_ref[branch >> 1]
    path_ref[2] = t3_ref[branch >> 2]


def features(xyz, centre):
    moved = (xyz - centre) * SCALE
    hi, lo = split(moved)
    exact = hi.astype(F32) + lo.astype(F32)
    norm = jnp.sum(exact * exact, axis=0, keepdims=True)
    n1 = norm.astype(BF16).astype(F32)
    n2 = (norm - n1).astype(BF16).astype(F32)
    n3 = norm - n1 - n2
    row = lax.broadcasted_iota(jnp.int32, xyz.shape, 0)
    norms = jnp.where(row == 0, n1, jnp.where(row == 1, n2, jnp.where(row == 2, n3, 0.0)))
    ones = jnp.where(row < 3, 1.0, 0.0)
    return hi.astype(F32), lo.astype(F32), norms, ones


def near_kernel(
    first, last, id_ref, near_ref, swap_a_ref, own_ref, swap_b_ref, out_ref, feat, rhs, target
):
    own_xyz = own_ref[16:24, :].astype(F32)
    low = jnp.min(own_xyz, axis=1, keepdims=True)
    high = jnp.max(own_xyz, axis=1, keepdims=True)
    centre = 0.5 * (low + high)
    for part, ref in enumerate((swap_a_ref, own_ref, swap_b_ref)):
        cols = pl.ds(part * 4096, 4096)
        rhs[:, cols] = ref[0:16, :]
        xyz = ref[16:24, :].astype(F32)
        hi, lo, norms, ones = features(xyz, centre)
        both = jnp.concatenate([hi, lo], axis=0).astype(BF16)
        feat[0:16, cols] = both
        feat[16:32, cols] = both
        feat[32:48, cols] = jnp.concatenate([ones, norms], axis=0).astype(BF16)
        if part == 1:
            for leaf in range(first, last):
                c = slice(leaf * 256, (leaf + 1) * 256)
                h = -2.0 * hi[:, c]
                m = -2.0 * lo[:, c]
                stack = jnp.concatenate([h, h, m, m, norms[:, c], ones[:, c]], axis=0)
                target[leaf - first] = jnp.transpose(stack).astype(BF16)
    base = (id_ref[0] - 1) * 16
    even = (id_ref[0] & 1) == 0

    def leaf_step(step, carry):
        left = target[step]
        total = jnp.zeros((16, 256), F32)
        for slot in range(8):
            source = near_ref[slot, first + step] - base
            source = jnp.minimum(jnp.maximum(source, 0), 47)
            part = source >> 4
            source = jnp.where(even, 2 - part, part) * 16 + (source & 15)
            cols = pl.ds(pl.multiple_of(source * 256, 256), 256)
            squared = jnp.maximum(dot(left, feat[:, cols], NN), 1e-20)
            tile = jnp.exp2(-(squared * lax.rsqrt(squared))).astype(BF16)
            total = total + dot(rhs[:, cols], tile, NT)
        out_ref[:, pl.ds(pl.multiple_of(step * 256, 256), 256)] = total
        return carry

    lax.fori_loop(0, last - first, leaf_step, 0, unroll=4)


def prep_kernel(
    id_ref, t1_hbm, t2_hbm, t3_hbm, fc_hbm, tc_hbm, packed_hbm, path_ref,
    packed, t1_ref, t2_ref, t3_ref, fc_ref, tc_ref, sems,
):
    moves = copies((t1_hbm, t2_hbm, t3_hbm, fc_hbm, tc_hbm), (t1_ref, t2_ref, t3_ref, fc_ref, tc_ref), sems)
    for move in moves:
        move.start()
    for move in moves:
        move.wait()
    prepare(id_ref, t1_ref, t2_ref, t3_ref, fc_ref, tc_ref, packed, path_ref)
    out = pltpu.make_async_copy(packed, packed_hbm.at[0:PACKED, :], sems.at[5])
    out.start()
    out.wait()


def prep_pass(dev, t1, t2, t3, fc, tc):
    return pl.pallas_call(
        prep_kernel,
        out_shape=[
            jax.ShapeDtypeStruct((ROOM, 128), BF16),
            jax.ShapeDtypeStruct((3, 64, 64), BF16),
        ],
        in_specs=smem(1) + hbm(5),
        out_specs=hbm(1) + vmem(1),
        scratch_shapes=[
            pltpu.VMEM((PACKED, 128), BF16),
            pltpu.VMEM((128, 64, 64), BF16),
            pltpu.VMEM((64, 64, 64), BF16),
            pltpu.VMEM((32, 64, 64), BF16),
            pltpu.VMEM((1, 16, 64, 64), BF16),
            pltpu.VMEM((1, 4, 8, 64, 64), BF16),
            pltpu.SemaphoreType.DMA((6,)),
        ],
        compiler_params=pltpu.CompilerParams(vmem_limit_bytes=GRANT),
        cost_estimate=pl.CostEstimate(flops=1_000_000, bytes_accessed=8_000_000, transcendentals=0),
        name="prep_pass",
    )(dev, t1, t2, t3, fc, tc)


def near_cost(leaves):
    return pl.CostEstimate(
        flops=400_000_000 * leaves, bytes_accessed=600_000, transcendentals=1_050_000 * leaves
    )


def near_scratch(leaves):
    return [
        pltpu.VMEM((48, 12288), BF16),
        pltpu.VMEM((16, 12288), BF16),
        pltpu.VMEM((leaves, 256, 48), BF16),
    ]


def near_field(dev, near_list, swap_a, own, swap_b, first, last):
    return pl.pallas_call(
        functools.partial(near_kernel, first, last),
        out_shape=jax.ShapeDtypeStruct((16, (last - first) * 256), F32),
        in_specs=smem(2) + vmem(3),
        out_specs=vmem(1)[0],
        scratch_shapes=near_scratch(last - first),
        compiler_params=pltpu.CompilerParams(vmem_limit_bytes=GRANT),
        cost_estimate=near_cost(last - first + 1),
        name="near_field",
    )(dev, near_list, swap_a, own, swap_b)


def mid_kernel(
    id_ref, flist_ref, fcount_ref, tlist_ref, own_ref, other_ref, packed_hbm,
    out_ref, shares_ref, nodes, packed, sem,
):
    move = pltpu.make_async_copy(packed_hbm.at[0:PACKED, :], packed, sem)
    move.start()
    my_core = (id_ref[0] >> 2) & 1
    lane16 = lax.broadcasted_iota(jnp.int32, (16, 128), 1)
    low16 = lane16 < 64
    half16 = jnp.where(low16, 0, 1)
    from_own = half16 == my_core

    def put(at, value):
        hi, lo = split(value)
        nodes[at] = jnp.concatenate([hi, lo], axis=0)

    def raise_four(pairs, weights):
        value = jnp.concatenate(pairs, axis=0)
        hi, lo = split(value)
        out = dot(jnp.concatenate([hi, lo], axis=0), weights, NT)
        out = out[:64] + out[64:]
        first = jnp.where(low16, out[0:16, 0:128], out[16:32, 0:128])
        second = jnp.where(low16, out[32:48, 128:256], out[48:64, 128:256])
        return first, second

    def side_by_side(first, count):
        return jnp.concatenate([packed[(first + k) * 64 : (first + k + 1) * 64, :] for k in range(count)], axis=1)

    ones = []
    for at_x in range(4):
        for z in range(16):
            at = (at_x * 64 + z) * 16
            sums = []
            for half in (own_ref, other_ref):
                parts = [half[y * 256 + at : y * 256 + at + 16, :].astype(F32) for y in range(4)]
                sums.append((parts[0] + parts[1]) + (parts[2] + parts[3]))
            ones.append(jnp.where(from_own, sums[0], sums[1]))
            put(at_x * 16 + z, ones[-1])
    move.wait()
    for at_x in range(4):
        twos = []
        for quad in range(4):
            node = at_x * 16 + quad * 4
            twos.extend(raise_four(ones[node : node + 4], packed[node * 64 : node * 64 + 256, :]))
        for k in range(8):
            put(64 + at_x * 8 + k, twos[k])
        threes = []
        for quad in range(2):
            row = (64 + at_x * 8 + quad * 4) * 64
            threes.extend(raise_four(twos[quad * 4 : quad * 4 + 4], packed[row : row + 256, :]))
        for k in range(4):
            put(96 + at_x * 4 + k, threes[k])
        row = (96 + at_x * 4) * 64
        fours = raise_four(threes, packed[row : row + 256, :])
        for k in range(2):
            put(112 + at_x * 2 + k, fours[k])

    blocks = []
    for slot in range(16):
        c = flist_ref[0, slot]
        c_y, c_core = c & 3, (c >> 2) & 1
        place = pl.multiple_of((((c >> 7) * 4 + c_y) * 16 + ((c >> 3) & 15)) * 16, 16)
        block = jnp.where(c_core == my_core, own_ref[pl.ds(place, 16), :], other_ref[pl.ds(place, 16), :])
        live = jnp.where(slot < fcount_ref[0], 1 - c_core, 2)
        blocks.append(block * jnp.where(half16 == live, 1.0, 0.0).astype(BF16))
    out_ref[16:32, :] = dot(jnp.concatenate(blocks, axis=1), side_by_side(112, 16), NT)

    parts = []
    for level, offset in enumerate((0, 64, 96, 112)):
        blocks = []
        for slot in range(8):
            node = tlist_ref[0, level, slot]
            block = nodes[offset + (node >> 1)]
            mask = jnp.where(half16 == (node & 1), 1.0, 0.0).astype(BF16)
            blocks.append(block * jnp.concatenate([mask, mask], axis=0))
        out = dot(jnp.concatenate(blocks, axis=1), side_by_side(128 + level * 8, 8), NT)
        parts.append(out[:16] + out[16:])
    out_ref[0:16, :] = parts[0]
    upper = jnp.concatenate([parts[1], parts[2]], axis=1)
    last = jnp.concatenate([parts[3], parts[3]], axis=1)
    for k in range(8):
        shares_ref[k, 0:16, :] = upper
        shares_ref[k, 16:32, :] = last


def mid_pass(dev, flist, fcount, tlist, own, other, packed):
    return pl.pallas_call(
        mid_kernel,
        out_shape=[
            jax.ShapeDtypeStruct((32, 64), F32),
            jax.ShapeDtypeStruct((8, 32, 128), F32),
        ],
        in_specs=smem(4) + vmem(2) + hbm(1),
        out_specs=vmem(2),
        scratch_shapes=[
            pltpu.VMEM((120, 32, 128), BF16),
            pltpu.VMEM((PACKED, 128), BF16),
            pltpu.SemaphoreType.DMA,
        ],
        compiler_params=pltpu.CompilerParams(vmem_limit_bytes=GRANT - 16 * 1024 * 1024),
        cost_estimate=pl.CostEstimate(flops=300_000_000, bytes_accessed=5_000_000, transcendentals=0),
        name="mid_pass",
    )(dev, flist, fcount, tlist, own, other, packed)


def down_kernel(
    id_ref, mid_hbm, shares_hbm, path_hbm, dt_hbm, lt_hbm, basis_hbm, near_a_hbm, near_b_hbm,
    out_ref, mid_ref, shares_ref, path_ref, dt_ref, lt_ref, basis_ref, near_a, near_b, sems,
):
    moves = copies(
        (mid_hbm, shares_hbm, path_hbm, dt_hbm, lt_hbm, basis_hbm, near_a_hbm, near_b_hbm),
        (mid_ref, shares_ref, path_ref, dt_ref, lt_ref, basis_ref, near_a, near_b),
        sems,
    )
    for move in moves:
        move.start()
    for move in moves[:4]:
        move.wait()
    zl = (id_ref[0] >> 3) & 3
    upper = jnp.zeros((16, 128), F32)
    down = jnp.zeros((16, 64), F32)
    low = lax.broadcasted_iota(jnp.int32, (16, 128), 1) < 64
    for o in range(8):
        pair = jnp.where((o >> 1) == zl, 1.0, 0.0)
        quad = jnp.where((o >> 2) == (zl >> 1), 1.0, 0.0)
        upper = upper + shares_ref[o, 0:16, :] * jnp.where(low, pair, quad)
        down = down + shares_ref[o, 16:32, 0:64]
    down = upper[:, 64:128] + wide_dot(down, path_ref[2], NN)
    down = upper[:, 0:64] + wide_dot(down, path_ref[1], NN)
    down = mid_ref[0:16, :] + wide_dot(down, path_ref[0], NN)
    down = mid_ref[16:32, :] + wide_dot(down, dt_ref[0], NN)
    for move in moves[4:]:
        move.wait()
    near_refs = (near_a, near_b)
    near_blocks = [(ref, k) for ref in near_refs for k in range(ref.shape[1] // 256)]
    for leaf in range(16):
        near_ref, k = near_blocks[leaf]
        leaf_down = wide_dot(down, lt_ref[leaf], NN).astype(BF16)
        cols = slice(leaf * 256, (leaf + 1) * 256)
        near = near_ref[:, k * 256 : (k + 1) * 256]
        out_ref[:, cols] = near + dot(leaf_down, basis_ref[leaf], NN)


def down_pass(dev, mid, shares, path, dt, lt, basis, near):
    return pl.pallas_call(
        down_kernel,
        out_shape=jax.ShapeDtypeStruct((16, 4096), F32),
        in_specs=smem(1) + hbm(8),
        out_specs=vmem(1)[0],
        scratch_shapes=[
            pltpu.VMEM((32, 64), F32),
            pltpu.VMEM((8, 32, 128), F32),
            pltpu.VMEM((3, 64, 64), BF16),
            pltpu.VMEM((1, 64, 64), BF16),
            pltpu.VMEM((16, 64, 64), BF16),
            pltpu.VMEM((16, 64, 256), BF16),
            pltpu.VMEM(near[0].shape, F32),
            pltpu.VMEM(near[1].shape, F32),
            pltpu.SemaphoreType.DMA((8,)),
        ],
        compiler_params=pltpu.CompilerParams(vmem_limit_bytes=GRANT),
        cost_estimate=pl.CostEstimate(flops=20_000_000, bytes_accessed=1_500_000, transcendentals=0),
        name="down_pass",
    )(dev, mid, shares, path, dt, lt, basis, *near)


def cyclic(value, axis, size, by):
    return lax.ppermute(value, axis, [(i, (i + by) % size) for i in range(size)])


def spread(value, axis, size):
    rows = value.shape[0]
    same = jnp.broadcast_to(value[None], (size, rows, 128))
    return lax.all_to_all(same, axis, 0, 0, tiled=True).reshape(size * rows, 128)


def on_device(
    rhs, coords, basis, lt, dt, t1, t2, t3, far_list, far_count, far_coupling, top_list, top_coupling,
    near_list,
):
    dev = lax.axis_index(DEV).astype(jnp.int32).reshape(1)
    tie = lax.optimization_barrier
    payload, own = up_pass(dev, rhs, coords, basis, lt, dt)
    blocks = lax.all_to_all(payload, ("zh", "zl"), 0, 0, tiled=True).reshape(256, 128)
    swap_a = lax.ppermute(own, DEV, [(i, i ^ 1) for i in range(512)])
    swap_b = lax.ppermute(own, DEV, [(i, ((i + 1) ^ 1) - 1) for i in range(1, 511)] + [(0, 511), (511, 0)])
    own, t1 = tie((own, t1))
    packed, path = prep_pass(dev, t1, t2, t3, far_coupling, top_coupling)
    blocks, swap_a, swap_b, packed = tie((blocks, swap_a, swap_b, packed))
    near_list = jnp.transpose(near_list)
    gathered = spread(blocks, ("x", "y"), 16)
    near_a = near_field(dev, near_list, swap_a, own, swap_b, 0, 8)
    gathered, near_a, packed = tie((gathered, near_a, packed))
    other = cyclic(gathered, "core", 2, 1)
    mid, shares = mid_pass(dev, far_list, far_count, top_list, gathered, other, packed)
    shares, dev_b = tie((shares, dev))
    near_b = near_field(dev_b, near_list, swap_a, own, swap_b, 8, 16)
    shares = lax.all_to_all(shares, ("zl", "core"), 0, 0, tiled=True)
    return down_pass(dev, mid, shares, path, dt, lt, basis, (near_a, near_b))


def solution(mesh):
    torus = Mesh(mesh.devices.reshape(4, 4, 4, 2, 4), DEV)
    branch = DEV[:4]
    in_specs = (
        P(None, DEV),
        P(None, DEV),
        P(DEV, None, None),
        P(DEV, None, None),
        P(DEV, None, None),
        P(),
        P(),
        P(),
        P(DEV, None),
        P(DEV),
        P(DEV, None, None, None),
        P(branch, None, None),
        P(branch, None, None, None, None),
        P(DEV, None),
    )
    return jax.shard_map(
        on_device, mesh=torus, in_specs=in_specs, out_specs=P(None, DEV), check_vma=False
    )
```

time: 384 us -> 87.9 us (0.23)
  blocking collectives: 128 us -> 0 us
  waiting for transfers between devices: 95.1 us -> 9.2 us
  local copies, waits for them, and re-layouts: 62.1 us -> 7.23 us
  matrix products: 45.3 us -> 0 us
  Pallas kernels: 0 us -> 30.5 us
  starting transfers between devices: 21.5 us -> 39.6 us
  other arithmetic: 14.7 us -> 0 us
  between operations: 14.4 us -> 0.78 us
    all_gather x1 -> x0, blocking collectives: 120 us -> none  [on_device(): all_one = lax.all_gather(level_one[None], 'branch', axis=0, tiled=True)]
    all_gather x1 -> x0, waiting for transfers between devices: 90.6 us -> none  [on_device(): lax.all_gather(coarse[None], ('branch', 'sub'), axis=0, tiled=True)]
    gather x37 -> x0, local copies, waits for them, and re-layouts: 56.4 us -> none  [the longest x16 24.7 us: near_leaf(): wide_rhs[:, sources]]
    dot_general x33 -> x0, matrix products: 45.3 us -> none  [the longest x16 23.7 us: near_leaf(): jnp.einsum('rjq,jpq->rp', wide_rhs[:, sources], tile_vals, preferred_elem...]
    pallas_call x0 -> x6, Pallas kernels: none -> 30.5 us  [the longest x2 15.3 us: near_field(): pl.pallas_call(functools.partial(near_kernel, first, last), out_shape=jax...]
    all_to_all x0 -> x3, starting transfers between devices: none -> 27.1 us  [the longest x1 15.8 us: on_device(): lax.all_to_all(payload, ('zh', 'zl'), 0, 0, tiled=True).reshape(256, 128)]
    reduce_sum x16 -> x0, other arithmetic: 10.6 us -> none  [kernel_tile(): squared = jnp.sum(spread_xyz * spread_xyz, axis=0)]
    ppermute x7 -> x3, starting transfers between devices: 21.5 us -> 12.5 us  [the longest x1 5.48 us: on_device(): lax.ppermute(own, DEV, [(i, (i + 1 ^ 1) - 1) for i in range(1, 511)] + [(...]
  transfers between devices with their start and end apart: 8 -> 6, of which waited for: 3 -> 2; matrix products, arithmetic and copies ran while one was open for 30% -> 5% of each run, Pallas kernels for 0% -> 23%
where the time goes in v1:
time: 87.9 us; the launch traced here: 87.3 us
  starting transfers between devices  39.6 us (45%)
  Pallas kernels  30.5 us (35%)
  waiting for transfers between devices  9.2 us (10%)
  local copies, waits for them, and re-layouts  7.23 us (8%)
    all_to_all x1, starting transfers between devices, on_device(): lax.all_to_all(payload, ('zh', 'zl'), 0, 0, tiled=True).reshape(256, 128)  15.8 us
    pallas_call x2, Pallas kernels, near_field(): pl.pallas_call(functools.partial(near_kernel, first, last), out_shape=jax...  15.3 us
    all_to_all x1, waiting for transfers between devices, spread(): lax.all_to_all(same, axis, 0, 0, tiled=True).reshape(size * rows, 128)  7.57 us
    all_to_all x1, starting transfers between devices, spread(): lax.all_to_all(same, axis, 0, 0, tiled=True).reshape(size * rows, 128)  6.3 us
    ppermute x1, starting transfers between devices, on_device(): lax.ppermute(own, DEV, [(i, (i + 1 ^ 1) - 1) for i in range(1, 511)] + [(...  5.48 us
    pallas_call x1, Pallas kernels, prep_pass(): pl.pallas_call(prep_kernel, out_shape=[jax.ShapeDtypeStruct((ROOM, 128),...  5.12 us
    ppermute x1, starting transfers between devices, cyclic(): lax.ppermute(value, axis, [(i, (i + by) % size) for i in range(size)])  5.1 us
    all_to_all x1, starting transfers between devices, on_device(): shares = lax.all_to_all(shares, ('zl', 'core'), 0, 0, tiled=True)  4.99 us
  transfers between devices with their start and end apart: 6, of which 2 were waited for; matrix products, arithmetic and copies ran while one was open for 5% of the time, Pallas kernels for 23%

profile of v1, /device:TPU:1, one launch (start us, length us, event | category | flops | bytes accessed | tf_op | source)
XLA Modules:
  0.0 87.3 jit_solution(535236471664563055)
XLA Ops:
  0.0 0.0 copy-start.1
  0.0 0.0 copy-start.2
  0.0 2.6 %up_pass.1 = (bf16[16,16,128]{2,1,0:T(8,128)(2,1)}, bf16[24,4096]{1,0:T(8,128)(2,1)}) custom-call(s32[1]{0:T(128)} %bitcast.id_ref, bf16[16,4096]{1,0:T(8,128)(2,1)} %rhs_hbm.1, bf16[3,4096]{1,0:T(4,128)(2,1)} %coords_hbm.1, bf16[16,64,256]{2,1,0:T(8,128)(2,1)} %basis_hbm.3, bf16[16,64,64]{2,1,0:T(8,128)(2,1)} %lt_hbm.3, bf16[1,64,64]{2,1,0:T(8,128)(2,1)} %dt_hbm.3), custom_call_target="tpu_custom_call" | custom-call | flops 20000000 | bytes 1000000 | tf_op jit(solution)/shard_map/up_pass/pallas_call | solution.py:88
  2.6 15.8 %all-to-all-start = ((bf16[16,16,128]{2,1,0:T(8,128)(2,1)}), bf16[16,16,128]{2,1,0:T(8,128)(2,1)S(1)}, u32[]{:S(2)}, u32[]{:S(2)}) async-start(bf16[16,16,128]{2,1,0:T(8,128)(2,1)} %get-tuple-element.22), calls=%async_computation | async-start | bytes 131072 | tf_op jit(solution)/shard_map/all_to_all | solution.py:437
  18.4 5.5 %collective-permute-start.1 = (bf16[24,4096]{1,0:T(8,128)(2,1)}, bf16[24,4096]{1,0:T(8,128)(2,1)S(1)}, u32[]{:S(2)}, u32[]{:S(2)}) collective-permute-start(bf16[24,4096]{1,0:T(8,128)(2,1)} %get-tuple-element.28.own_ref), channel_id=1, source_target_pairs={{1,2},{2,1},{3,4},{4,3},{5,6},{6,5},{7,8},{8,7},{9,10},{10,9},{11,... | collective-permute-start | bytes 589832 | tf_op jit(solution)/shard_map/ppermute | solution.py:439
  23.8 1.9 %collective-permute-start = (bf16[24,4096]{1,0:T(8,128)(2,1)}, bf16[24,4096]{1,0:T(8,128)(2,1)S(1)}, u32[]{:S(2)}, u32[]{:S(2)}) collective-permute-start(bf16[24,4096]{1,0:T(8,128)(2,1)} %get-tuple-element.28.own_ref), channel_id=1, source_target_pairs={{0,1},{1,0},{2,3},{3,2},{4,5},{5,4},{6,7},{7,6},{8,9},{9,8},{10,11... | collective-permute-start | bytes 589832 | tf_op jit(solution)/shard_map/ppermute | solution.py:438
  25.8 4.7 %copy.15.t1_hbm = bf16[128,64,64]{2,1,0:T(8,128)(2,1)} copy(bf16[128,64,64]{0,2,1:T(8,128)(2,1)} %param.19) | data formatting | bytes 2097152 | tf_op jit(solution)/shard_map/optimization_barrier | solution.py:440
  30.5 5.1 %prep_pass.1 = (bf16[98304,128]{1,0:T(8,128)(2,1)}, bf16[3,64,64]{2,1,0:T(8,128)(2,1)}) custom-call(s32[1]{0:T(128)} %bitcast.id_ref, bf16[128,64,64]{2,1,0:T(8,128)(2,1)} %copy.15.t1_hbm, bf16[64,64,64]{2,1,0:T(8,128)(2,1)} %t2_hbm.1, bf16[32,64,64]{2,1,0:T(8,128)(2,1)} %t3_hbm.1, bf16[1,16,64,64]{3,2,1,0:T(8,128)(2,1)} %fc_hbm.1, ...), custom_call_target="tpu_custom_call" | custom-call | flops 1000000 | bytes 8000000 | tf_op jit(solution)/shard_map/prep_pass/pallas_call | solution.py:204
  35.6 0.0 collective-permute-done.1.swap_b_ref
  35.6 0.0 copy-start.4
  35.6 0.0 collective-permute-done.swap_a_ref
  35.7 0.0 copy-start.5
  35.7 0.0 all-to-all-done
  35.7 1.3 %broadcast_in_dim.2 = bf16[16,256,128]{2,1,0:T(8,128)(2,1)} broadcast(bf16[256,128]{1,0:T(8,128)(2,1)S(1)} %bitcast.6), dimensions={1,2} | broadcast | bytes 1114112 | tf_op jit(solution)/shard_map/broadcast_in_dim | solution.py:426
  36.9 6.3 %all-to-all-start.1 = ((bf16[16,256,128]{2,1,0:T(8,128)(2,1)}), bf16[16,256,128]{2,1,0:T(8,128)(2,1)S(1)}, u32[]{:S(2)}, u32[]{:S(2)}) async-start(bf16[16,256,128]{2,1,0:T(8,128)(2,1)} %broadcast_in_dim.2), calls=%async_computation.1 | async-start | bytes 2097152 | tf_op jit(solution)/shard_map/all_to_all | solution.py:427
  43.2 0.0 copy-done.4
  43.3 0.0 copy-done.5
  43.3 7.6 %near_field.2.near_a_hbm = f32[16,2048]{1,0:T(8,128)} custom-call(s32[1]{0:T(128)} %bitcast.id_ref, s32[8,16]{1,0:T(8,128)} %bitcast.7, bf16[24,4096]{1,0:T(8,128)(2,1)} %copy-done.5, bf16[24,4096]{1,0:T(8,128)(2,1)} %get-tuple-element.28.own_ref, bf16[24,4096]{1,0:T(8,128)(2,1)} %copy-done.4), custom_call_target="tpu_custom_call" | custom-call | flops 3600000000 | bytes 600000 | tf_op jit(solution)/shard_map/near_field/pallas_call | solution.py:242
  50.9 7.6 %all-to-all-done.1 = bf16[16,256,128]{2,1,0:T(8,128)(2,1)S(1)} async-done(((bf16[16,256,128]{2,1,0:T(8,128)(2,1)}), bf16[16,256,128]{2,1,0:T(8,128)(2,1)S(1)}, u32[]{:S(2)}, u32[]{:S(2)}) %all-to-all-start.1) | async-done | bytes 1048608 | tf_op jit(solution)/shard_map/all_to_all | solution.py:427
  58.5 5.1 %collective-permute-start.2 = (bf16[4096,128]{1,0:T(8,128)(2,1)S(1)}, bf16[4096,128]{1,0:T(8,128)(2,1)S(1)}, u32[]{:S(2)}, u32[]{:S(2)}) collective-permute-start(bf16[4096,128]{1,0:T(8,128)(2,1)S(1)} %bitcast.4), channel_id=1, source_target_pairs={{0,4},{4,0},{1,5},{5,1},{2,6},{6,2},{3,7},{7,3},{8,12},{12,8},{9,1... | collective-permute-start | bytes 3145736 | tf_op jit(solution)/shard_map/ppermute | solution.py:421
  64.2 1.6 %collective-permute-done.2.other_ref = bf16[4096,128]{1,0:T(8,128)(2,1)S(1)} collective-permute-done((bf16[4096,128]{1,0:T(8,128)(2,1)S(1)}, bf16[4096,128]{1,0:T(8,128)(2,1)S(1)}, u32[]{:S(2)}, u32[]{:S(2)}) %collective-permute-start.2) | collective-permute-done | bytes 1048608 | tf_op jit(solution)/shard_map/ppermute | solution.py:421
  65.8 0.0 copy-done.1
  65.8 0.0 copy-done.2
  65.8 4.9 %mid_pass.1 = (f32[32,64]{1,0:T(8,128)S(1)}, f32[8,32,128]{2,1,0:T(8,128)}) custom-call(s32[1]{0:T(128)} %bitcast.id_ref, s32[1,16]{1,0:T(1,128)S(1)} %copy-done.2, s32[1]{0:T(128)S(6)} %copy.16.fcount_ref, s32[1,4,8]{2,1,0:T(4,128)S(1)} %copy-done.1, bf16[4096,128]{1,0:T(8,128)(2,1)S(1)} %bitcast.5, bf16[4096,128]{1,0:T(8,128)(2,1)S(1)} %collective-permute-done.2.other_ref, ...), custom_call_target="tpu_custom_call" | custom-call | flops 300000000 | bytes 5000000 | tf_op jit(solution)/shard_map/mid_pass/pallas_call | solution.py:340
  70.7 0.0 copy-start
  70.7 0.6 copy-done
  71.3 5.0 %all-to-all-start.2 = ((f32[8,32,128]{2,1,0:T(8,128)}), f32[8,32,128]{2,1,0:T(8,128)S(1)}, u32[]{:S(2)}, u32[]{:S(2)}) async-start(f32[8,32,128]{2,1,0:T(8,128)} %get-tuple-element.35), calls=%async_computation.2 | async-start | bytes 262144 | tf_op jit(solution)/shard_map/all_to_all | solution.py:451
  76.3 7.6 %near_field.3.near_b_hbm = f32[16,2048]{1,0:T(8,128)} custom-call(s32[1]{0:T(128)} %bitcast.id_ref, s32[8,16]{1,0:T(8,128)} %bitcast.8, bf16[24,4096]{1,0:T(8,128)(2,1)} %copy-done.5, bf16[24,4096]{1,0:T(8,128)(2,1)} %get-tuple-element.28.own_ref, bf16[24,4096]{1,0:T(8,128)(2,1)} %copy-done.4), custom_call_target="tpu_custom_call" | custom-call | flops 3600000000 | bytes 600000 | tf_op jit(solution)/shard_map/near_field/pallas_call | solution.py:242
  84.0 0.0 all-to-all-done.2.shares_hbm
  84.0 0.0 copy-start.3
  84.0 0.6 copy-done.3
  84.6 2.7 %down_pass.1 = f32[16,4096]{1,0:T(8,128)} custom-call(s32[1]{0:T(128)} %bitcast.id_ref, f32[32,64]{1,0:T(8,128)} %copy-done, f32[8,32,128]{2,1,0:T(8,128)} %copy-done.3, bf16[3,64,64]{2,1,0:T(8,128)(2,1)} %get-tuple-element.36.path_hbm, bf16[1,64,64]{2,1,0:T(8,128)(2,1)} %dt_hbm.3, bf16[16,64,64]{2,1,0:T(8,128)(2,1)} %lt_hbm.3, ...), custom_call_target="tpu_custom_call" | custom-call | flops 20000000 | bytes 1500000 | tf_op jit(solution)/shard_map/down_pass/pallas_call | solution.py:398
Async XLA Ops:
  0.0 65.8 %copy-start.1 = (s32[1,4,8]{2,1,0:T(4,128)S(1)}, s32[1,4,8]{2,1,0:T(4,128)}, u32[]{:S(2)}) copy-start(s32[1,4,8]{2,1,0:T(4,128)} %tlist_ref.1) | copy-start | bytes 388
  0.0 65.8 %copy-start.2 = (s32[1,16]{1,0:T(1,128)S(1)}, s32[1,16]{1,0:T(1,128)}, u32[]{:S(2)}) copy-start(s32[1,16]{1,0:T(1,128)} %flist_ref.1) | copy-start | bytes 196
  2.6 33.1 %all-to-all-start = ((bf16[16,16,128]{2,1,0:T(8,128)(2,1)}), bf16[16,16,128]{2,1,0:T(8,128)(2,1)S(1)}, u32[]{:S(2)}, u32[]{:S(2)}) async-start(bf16[16,16,128]{2,1,0:T(8,128)(2,1)} %get-tuple-element.22), calls=%async_computation | async-start | bytes 131072 | tf_op jit(solution)/shard_map/all_to_all | solution.py:437
  18.4 17.3 %collective-permute-start.1 = (bf16[24,4096]{1,0:T(8,128)(2,1)}, bf16[24,4096]{1,0:T(8,128)(2,1)S(1)}, u32[]{:S(2)}, u32[]{:S(2)}) collective-permute-start(bf16[24,4096]{1,0:T(8,128)(2,1)} %get-tuple-element.28.own_ref), channel_id=1, source_target_pairs={{1,2},{2,1},{3,4},{4,3},{5,6},{6,5},{7,8},{8,7},{9,10},{10,9},{11,... | collective-permute-start | bytes 589832 | tf_op jit(solution)/shard_map/ppermute | solution.py:439
  23.8 11.8 %collective-permute-start = (bf16[24,4096]{1,0:T(8,128)(2,1)}, bf16[24,4096]{1,0:T(8,128)(2,1)S(1)}, u32[]{:S(2)}, u32[]{:S(2)}) collective-permute-start(bf16[24,4096]{1,0:T(8,128)(2,1)} %get-tuple-element.28.own_ref), channel_id=1, source_target_pairs={{0,1},{1,0},{2,3},{3,2},{4,5},{5,4},{6,7},{7,6},{8,9},{9,8},{10,11... | collective-permute-start | bytes 589832 | tf_op jit(solution)/shard_map/ppermute | solution.py:438
  35.6 7.6 %copy-start.4 = (bf16[24,4096]{1,0:T(8,128)(2,1)}, bf16[24,4096]{1,0:T(8,128)(2,1)S(1)}, u32[]{:S(2)}) copy-start(bf16[24,4096]{1,0:T(8,128)(2,1)S(1)} %collective-permute-done.1.swap_b_ref) | copy-start | bytes 589828
  35.7 7.6 %copy-start.5 = (bf16[24,4096]{1,0:T(8,128)(2,1)}, bf16[24,4096]{1,0:T(8,128)(2,1)S(1)}, u32[]{:S(2)}) copy-start(bf16[24,4096]{1,0:T(8,128)(2,1)S(1)} %collective-permute-done.swap_a_ref) | copy-start | bytes 589828
  36.9 21.5 %all-to-all-start.1 = ((bf16[16,256,128]{2,1,0:T(8,128)(2,1)}), bf16[16,256,128]{2,1,0:T(8,128)(2,1)S(1)}, u32[]{:S(2)}, u32[]{:S(2)}) async-start(bf16[16,256,128]{2,1,0:T(8,128)(2,1)} %broadcast_in_dim.2), calls=%async_computation.1 | async-start | bytes 2097152 | tf_op jit(solution)/shard_map/all_to_all | solution.py:427
  58.5 7.4 %collective-permute-start.2 = (bf16[4096,128]{1,0:T(8,128)(2,1)S(1)}, bf16[4096,128]{1,0:T(8,128)(2,1)S(1)}, u32[]{:S(2)}, u32[]{:S(2)}) collective-permute-start(bf16[4096,128]{1,0:T(8,128)(2,1)S(1)} %bitcast.4), channel_id=1, source_target_pairs={{0,4},{4,0},{1,5},{5,1},{2,6},{6,2},{3,7},{7,3},{8,12},{12,8},{9,1... | collective-permute-start | bytes 3145736 | tf_op jit(solution)/shard_map/ppermute | solution.py:421
  70.7 0.6 copy-start
  71.3 12.6 %all-to-all-start.2 = ((f32[8,32,128]{2,1,0:T(8,128)}), f32[8,32,128]{2,1,0:T(8,128)S(1)}, u32[]{:S(2)}, u32[]{:S(2)}) async-start(f32[8,32,128]{2,1,0:T(8,128)} %get-tuple-element.35), calls=%async_computation.2 | async-start | bytes 262144 | tf_op jit(solution)/shard_map/all_to_all | solution.py:451
  84.0 0.6 copy-start.3

commit v2 on v1

--- a/solution.py
+++ b/solution.py
@@ -122,9 +122,27 @@
         for slot in range(8):
             put(128 + level * 8 + slot, tc_ref[0, level, slot], tc_ref[0, level, slot])
     branch = id_ref[0] >> 2
-    path_ref[0] = t1_ref[branch]
-    path_ref[1] = t2_ref[branch >> 1]
-    path_ref[2] = t3_ref[branch >> 2]
+    path_ref[0] = t2_ref[branch >> 1]
+    path_ref[1] = t3_ref[branch >> 2]
+
+
+def pick_kernel(id_ref, t1_hbm, out_hbm, sem):
+    move = pltpu.make_async_copy(t1_hbm.at[pl.ds(id_ref[0] >> 2, 1)], out_hbm, sem)
+    move.start()
+    move.wait()
+
+
+def pick_pass(dev, t1):
+    return pl.pallas_call(
+        pick_kernel,
+        out_shape=jax.ShapeDtypeStruct((1, 64, 64), BF16),
+        in_specs=smem(1) + hbm(1),
+        out_specs=hbm(1)[0],
+        scratch_shapes=[pltpu.SemaphoreType.DMA],
+        compiler_params=pltpu.CompilerParams(vmem_limit_bytes=GRANT),
+        cost_estimate=pl.CostEstimate(flops=0, bytes_accessed=32_000, transcendentals=0),
+        name="pick_pass",
+    )(dev, t1)
 
 
 def features(xyz, centre):
@@ -142,7 +160,7 @@
 
 
 def near_kernel(
-    first, last, id_ref, near_ref, swap_a_ref, own_ref, swap_b_ref, out_ref, feat, rhs, target
+    first, last, id_ref, near_ref, swap_a_ref, own_ref, swap_b_ref, out_ref, feat, rhs, target, between=None
 ):
     own_xyz = own_ref[16:24, :].astype(F32)
     low = jnp.min(own_xyz, axis=1, keepdims=True)
@@ -164,6 +182,8 @@
                 m = -2.0 * lo[:, c]
                 stack = jnp.concatenate([h, h, m, m, norms[:, c], ones[:, c]], axis=0)
                 target[leaf - first] = jnp.transpose(stack).astype(BF16)
+    if between is not None:
+        between()
     base = (id_ref[0] - 1) * 16
     even = (id_ref[0] & 1) == 0
 
@@ -185,31 +205,54 @@
     lax.fori_loop(0, last - first, leaf_step, 0, unroll=4)
 
 
-def prep_kernel(
-    id_ref, t1_hbm, t2_hbm, t3_hbm, fc_hbm, tc_hbm, packed_hbm, path_ref,
-    packed, t1_ref, t2_ref, t3_ref, fc_ref, tc_ref, sems,
+def near_and_prep_kernel(
+    first, last, id_ref, near_ref, swap_a_ref, own_ref, swap_b_ref, t1_hbm, t2_hbm, t3_hbm, fc_hbm, tc_hbm,
+    out_ref, packed_hbm, path_ref,
+    feat, rhs, target, packed, t1_ref, t2_ref, t3_ref, fc_ref, tc_ref, sems,
 ):
     moves = copies((t1_hbm, t2_hbm, t3_hbm, fc_hbm, tc_hbm), (t1_ref, t2_ref, t3_ref, fc_ref, tc_ref), sems)
+    out = pltpu.make_async_copy(packed, packed_hbm.at[0:PACKED, :], sems.at[5])
     for move in moves:
         move.start()
-    for move in moves:
-        move.wait()
-    prepare(id_ref, t1_ref, t2_ref, t3_ref, fc_ref, tc_ref, packed, path_ref)
-    out = pltpu.make_async_copy(packed, packed_hbm.at[0:PACKED, :], sems.at[5])
-    out.start()
+
+    def between():
+        for move in moves:
+            move.wait()
+        prepare(id_ref, t1_ref, t2_ref, t3_ref, fc_ref, tc_ref, packed, path_ref)
+        out.start()
+
+    near_kernel(
+        first, last, id_ref, near_ref, swap_a_ref, own_ref, swap_b_ref, out_ref, feat, rhs, target, between
+    )
     out.wait()
 
 
-def prep_pass(dev, t1, t2, t3, fc, tc):
-    return pl.pallas_call(
-        prep_kernel,
+def near_cost(leaves):
+    return pl.CostEstimate(
+        flops=400_000_000 * leaves, bytes_accessed=600_000, transcendentals=1_050_000 * leaves
+    )
+
+
+def near_scratch(leaves):
+    return [
+        pltpu.VMEM((48, 12288), BF16),
+        pltpu.VMEM((16, 12288), BF16),
+        pltpu.VMEM((leaves, 256, 48), BF16),
+    ]
+
+
+def near_and_prep(dev, near_list, swap_a, own, swap_b, t1, t2, t3, fc, tc, first, last):
+    return pl.pallas_call(
+        functools.partial(near_and_prep_kernel, first, last),
         out_shape=[
+            jax.ShapeDtypeStruct((16, (last - first) * 256), F32),
             jax.ShapeDtypeStruct((ROOM, 128), BF16),
-            jax.ShapeDtypeStruct((3, 64, 64), BF16),
-        ],
-        in_specs=smem(1) + hbm(5),
-        out_specs=hbm(1) + vmem(1),
-        scratch_shapes=[
+            jax.ShapeDtypeStruct((2, 64, 64), BF16),
+        ],
+        in_specs=smem(2) + vmem(3) + hbm(5),
+        out_specs=vmem(1) + hbm(1) + vmem(1),
+        scratch_shapes=near_scratch(last - first)
+        + [
             pltpu.VMEM((PACKED, 128), BF16),
             pltpu.VMEM((128, 64, 64), BF16),
             pltpu.VMEM((64, 64, 64), BF16),
@@ -219,23 +262,9 @@
             pltpu.SemaphoreType.DMA((6,)),
         ],
         compiler_params=pltpu.CompilerParams(vmem_limit_bytes=GRANT),
-        cost_estimate=pl.CostEstimate(flops=1_000_000, bytes_accessed=8_000_000, transcendentals=0),
-        name="prep_pass",
-    )(dev, t1, t2, t3, fc, tc)
-
-
-def near_cost(leaves):
-    return pl.CostEstimate(
-        flops=400_000_000 * leaves, bytes_accessed=600_000, transcendentals=1_050_000 * leaves
-    )
-
-
-def near_scratch(leaves):
-    return [
-        pltpu.VMEM((48, 12288), BF16),
-        pltpu.VMEM((16, 12288), BF16),
-        pltpu.VMEM((leaves, 256, 48), BF16),
-    ]
+        cost_estimate=near_cost(last - first + 2),
+        name="near_and_prep",
+    )(dev, near_list, swap_a, own, swap_b, t1, t2, t3, fc, tc)
 
 
 def near_field(dev, near_list, swap_a, own, swap_b, first, last):
@@ -251,12 +280,35 @@
     )(dev, near_list, swap_a, own, swap_b)
 
 
+def half_kernel(own_ref, packed_hbm, sums_ref, packed_ref, sem):
+    move = pltpu.make_async_copy(packed_hbm.at[0:PACKED, :], packed_ref, sem)
+    move.start()
+    for x in range(4):
+        parts = [own_ref[(x * 4 + y) * 256 : (x * 4 + y + 1) * 256, :].astype(F32) for y in range(4)]
+        sums_ref[x * 256 : (x + 1) * 256, :] = (parts[0] + parts[1]) + (parts[2] + parts[3])
+    move.wait()
+
+
+def half_pass(own, packed):
+    return pl.pallas_call(
+        half_kernel,
+        out_shape=[
+            jax.ShapeDtypeStruct((1024, 128), F32),
+            jax.ShapeDtypeStruct((PACKED, 128), BF16),
+        ],
+        in_specs=vmem(1) + hbm(1),
+        out_specs=vmem(2),
+        scratch_shapes=[pltpu.SemaphoreType.DMA],
+        compiler_params=pltpu.CompilerParams(vmem_limit_bytes=GRANT - 16 * 1024 * 1024),
+        cost_estimate=pl.CostEstimate(flops=1_000_000, bytes_accessed=5_000_000, transcendentals=0),
+        name="half_pass",
+    )(own, packed)
+
+
 def mid_kernel(
-    id_ref, flist_ref, fcount_ref, tlist_ref, own_ref, other_ref, packed_hbm,
-    out_ref, shares_ref, nodes, packed, sem,
-):
-    move = pltpu.make_async_copy(packed_hbm.at[0:PACKED, :], packed, sem)
-    move.start()
+    id_ref, flist_ref, fcount_ref, tlist_ref, own_ref, other_ref, sums_ref, packed,
+    out_ref, shares_ref, nodes,
+):
     my_core = (id_ref[0] >> 2) & 1
     lane16 = lax.broadcasted_iota(jnp.int32, (16, 128), 1)
     low16 = lane16 < 64
@@ -283,13 +335,11 @@
     for at_x in range(4):
         for z in range(16):
             at = (at_x * 64 + z) * 16
-            sums = []
-            for half in (own_ref, other_ref):
-                parts = [half[y * 256 + at : y * 256 + at + 16, :].astype(F32) for y in range(4)]
-                sums.append((parts[0] + parts[1]) + (parts[2] + parts[3]))
-            ones.append(jnp.where(from_own, sums[0], sums[1]))
+            parts = [other_ref[y * 256 + at : y * 256 + at + 16, :].astype(F32) for y in range(4)]
+            other = (parts[0] + parts[1]) + (parts[2] + parts[3])
+            row = (at_x * 16 + z) * 16
+            ones.append(jnp.where(from_own, sums_ref[row : row + 16, :], other))
             put(at_x * 16 + z, ones[-1])
-    move.wait()
     for at_x in range(4):
         twos = []
         for quad in range(4):
@@ -336,38 +386,34 @@
         shares_ref[k, 16:32, :] = last
 
 
-def mid_pass(dev, flist, fcount, tlist, own, other, packed):
+def mid_pass(dev, flist, fcount, tlist, own, other, sums, packed):
     return pl.pallas_call(
         mid_kernel,
         out_shape=[
             jax.ShapeDtypeStruct((32, 64), F32),
             jax.ShapeDtypeStruct((8, 32, 128), F32),
         ],
-        in_specs=smem(4) + vmem(2) + hbm(1),
+        in_specs=smem(4) + vmem(4),
         out_specs=vmem(2),
-        scratch_shapes=[
-            pltpu.VMEM((120, 32, 128), BF16),
-            pltpu.VMEM((PACKED, 128), BF16),
-            pltpu.SemaphoreType.DMA,
-        ],
+        scratch_shapes=[pltpu.VMEM((120, 32, 128), BF16)],
         compiler_params=pltpu.CompilerParams(vmem_limit_bytes=GRANT - 16 * 1024 * 1024),
         cost_estimate=pl.CostEstimate(flops=300_000_000, bytes_accessed=5_000_000, transcendentals=0),
         name="mid_pass",
-    )(dev, flist, fcount, tlist, own, other, packed)
+    )(dev, flist, fcount, tlist, own, other, sums, packed)
 
 
 def down_kernel(
-    id_ref, mid_hbm, shares_hbm, path_hbm, dt_hbm, lt_hbm, basis_hbm, near_a_hbm, near_b_hbm,
-    out_ref, mid_ref, shares_ref, path_ref, dt_ref, lt_ref, basis_ref, near_a, near_b, sems,
+    id_ref, mid_hbm, shares_hbm, path_hbm, one_hbm, dt_hbm, lt_hbm, basis_hbm, near_a_hbm, near_b_hbm,
+    out_ref, mid_ref, shares_ref, path_ref, one_ref, dt_ref, lt_ref, basis_ref, near_a, near_b, sems,
 ):
     moves = copies(
-        (mid_hbm, shares_hbm, path_hbm, dt_hbm, lt_hbm, basis_hbm, near_a_hbm, near_b_hbm),
-        (mid_ref, shares_ref, path_ref, dt_ref, lt_ref, basis_ref, near_a, near_b),
+        (mid_hbm, shares_hbm, path_hbm, one_hbm, dt_hbm, lt_hbm, basis_hbm, near_a_hbm, near_b_hbm),
+        (mid_ref, shares_ref, path_ref, one_ref, dt_ref, lt_ref, basis_ref, near_a, near_b),
         sems,
     )
     for move in moves:
         move.start()
-    for move in moves[:4]:
+    for move in moves[:5]:
         move.wait()
     zl = (id_ref[0] >> 3) & 3
     upper = jnp.zeros((16, 128), F32)
@@ -378,11 +424,11 @@
         quad = jnp.where((o >> 2) == (zl >> 1), 1.0, 0.0)
         upper = upper + shares_ref[o, 0:16, :] * jnp.where(low, pair, quad)
         down = down + shares_ref[o, 16:32, 0:64]
-    down = upper[:, 64:128] + wide_dot(down, path_ref[2], NN)
-    down = upper[:, 0:64] + wide_dot(down, path_ref[1], NN)
-    down = mid_ref[0:16, :] + wide_dot(down, path_ref[0], NN)
+    down = upper[:, 64:128] + wide_dot(down, path_ref[1], NN)
+    down = upper[:, 0:64] + wide_dot(down, path_ref[0], NN)
+    down = mid_ref[0:16, :] + wide_dot(down, one_ref[0], NN)
     down = mid_ref[16:32, :] + wide_dot(down, dt_ref[0], NN)
-    for move in moves[4:]:
+    for move in moves[5:]:
         move.wait()
     near_refs = (near_a, near_b)
     near_blocks = [(ref, k) for ref in near_refs for k in range(ref.shape[1] // 256)]
@@ -394,27 +440,28 @@
         out_ref[:, cols] = near + dot(leaf_down, basis_ref[leaf], NN)
 
 
-def down_pass(dev, mid, shares, path, dt, lt, basis, near):
+def down_pass(dev, mid, shares, path, one, dt, lt, basis, near):
     return pl.pallas_call(
         down_kernel,
         out_shape=jax.ShapeDtypeStruct((16, 4096), F32),
-        in_specs=smem(1) + hbm(8),
+        in_specs=smem(1) + hbm(9),
         out_specs=vmem(1)[0],
         scratch_shapes=[
             pltpu.VMEM((32, 64), F32),
             pltpu.VMEM((8, 32, 128), F32),
-            pltpu.VMEM((3, 64, 64), BF16),
+            pltpu.VMEM((2, 64, 64), BF16),
+            pltpu.VMEM((1, 64, 64), BF16),
             pltpu.VMEM((1, 64, 64), BF16),
             pltpu.VMEM((16, 64, 64), BF16),
             pltpu.VMEM((16, 64, 256), BF16),
             pltpu.VMEM(near[0].shape, F32),
             pltpu.VMEM(near[1].shape, F32),
-            pltpu.SemaphoreType.DMA((8,)),
+            pltpu.SemaphoreType.DMA((9,)),
         ],
         compiler_params=pltpu.CompilerParams(vmem_limit_bytes=GRANT),
         cost_estimate=pl.CostEstimate(flops=20_000_000, bytes_accessed=1_500_000, transcendentals=0),
         name="down_pass",
-    )(dev, mid, shares, path, dt, lt, basis, *near)
+    )(dev, mid, shares, path, one, dt, lt, basis, *near)
 
 
 def cyclic(value, axis, size, by):
@@ -438,18 +485,21 @@
     swap_a = lax.ppermute(own, DEV, [(i, i ^ 1) for i in range(512)])
     swap_b = lax.ppermute(own, DEV, [(i, ((i + 1) ^ 1) - 1) for i in range(1, 511)] + [(0, 511), (511, 0)])
     own, t1 = tie((own, t1))
-    packed, path = prep_pass(dev, t1, t2, t3, far_coupling, top_coupling)
-    blocks, swap_a, swap_b, packed = tie((blocks, swap_a, swap_b, packed))
+    one = pick_pass(dev, t1)
+    blocks, swap_a, swap_b, one = tie((blocks, swap_a, swap_b, one))
     near_list = jnp.transpose(near_list)
     gathered = spread(blocks, ("x", "y"), 16)
-    near_a = near_field(dev, near_list, swap_a, own, swap_b, 0, 8)
+    near_a, packed, path = near_and_prep(
+        dev, near_list, swap_a, own, swap_b, t1, t2, t3, far_coupling, top_coupling, 0, 12
+    )
     gathered, near_a, packed = tie((gathered, near_a, packed))
     other = cyclic(gathered, "core", 2, 1)
-    mid, shares = mid_pass(dev, far_list, far_count, top_list, gathered, other, packed)
+    sums, packed = half_pass(gathered, packed)
+    mid, shares = mid_pass(dev, far_list, far_count, top_list, gathered, other, sums, packed)
     shares, dev_b = tie((shares, dev))
-    near_b = near_field(dev_b, near_list, swap_a, own, swap_b, 8, 16)
+    near_b = near_field(dev_b, near_list, swap_a, own, swap_b, 12, 16)
     shares = lax.all_to_all(shares, ("zl", "core"), 0, 0, tiled=True)
-    return down_pass(dev, mid, shares, path, dt, lt, basis, (near_a, near_b))
+    return down_pass(dev, mid, shares, path, one, dt, lt, basis, (near_a, near_b))
 
 
 def solution(mesh):

time: 87.9 us -> 83.2 us (0.947)
  waiting for transfers between devices: 9.2 us -> 3.59 us
  starting transfers between devices: 39.6 us -> 41.8 us
  Pallas kernels: 30.5 us -> 29.2 us
    pallas_call x1 -> x3, Pallas kernels: 5.12 us -> 15.9 us  [the longest x1 12.5 us: near_and_prep(): pl.pallas_call(functools.partial(near_and_prep_kernel, first, last), out_...]
    pallas_call x2 -> x1, Pallas kernels: 15.3 us -> 4.89 us  [near_field(): pl.pallas_call(functools.partial(near_kernel, first, last), out_shape=jax...]
    all_to_all x1, waiting for transfers between devices: 7.57 us -> 2.65 us  [spread(): lax.all_to_all(same, axis, 0, 0, tiled=True).reshape(size * rows, 128)]
    all_to_all x1, starting transfers between devices: 4.99 us -> 6.82 us  [on_device(): shares = lax.all_to_all(shares, ('zl', 'core'), 0, 0, tiled=True)]
    pallas_call x1, Pallas kernels: 4.87 us -> 3.16 us  [mid_pass(): pl.pallas_call(mid_kernel, out_shape=[jax.ShapeDtypeStruct((32, 64), F32)...]
    ppermute x1, waiting for transfers between devices: 1.62 us -> 0.01 us  [cyclic(): lax.ppermute(value, axis, [(i, (i + by) % size) for i in range(size)])]
    ppermute x1, starting transfers between devices: 1.92 us -> 3.2 us  [on_device(): swap_a = lax.ppermute(own, DEV, [(i, i ^ 1) for i in range(512)])]
    all_to_all x1, waiting for transfers between devices: 0.01 us -> 0.92 us  [on_device(): shares = lax.all_to_all(shares, ('zl', 'core'), 0, 0, tiled=True)]
  transfers between devices with their start and end apart: 6 -> 6, of which waited for: 2 -> 2; matrix products, arithmetic and copies ran while one was open for 5% -> 6% of each run, Pallas kernels for 23% -> 25%
where the time goes in v2:
time: 83.2 us; the launch traced here: 82.6 us
  starting transfers between devices  41.8 us (50%)
  Pallas kernels  29.2 us (35%)
  local copies, waits for them, and re-layouts  7.19 us (9%)
  waiting for transfers between devices  3.59 us (4%)
    all_to_all x1, starting transfers between devices, on_device(): lax.all_to_all(payload, ('zh', 'zl'), 0, 0, tiled=True).reshape(256, 128)  15.8 us
    pallas_call x1, Pallas kernels, near_and_prep(): pl.pallas_call(functools.partial(near_and_prep_kernel, first, last), out_...  12.5 us
    all_to_all x1, starting transfers between devices, on_device(): shares = lax.all_to_all(shares, ('zl', 'core'), 0, 0, tiled=True)  6.82 us
    all_to_all x1, starting transfers between devices, spread(): lax.all_to_all(same, axis, 0, 0, tiled=True).reshape(size * rows, 128)  5.97 us
    ppermute x1, starting transfers between devices, cyclic(): lax.ppermute(value, axis, [(i, (i + by) % size) for i in range(size)])  5.11 us
    ppermute x1, starting transfers between devices, on_device(): lax.ppermute(own, DEV, [(i, (i + 1 ^ 1) - 1) for i in range(1, 511)] + [(...  4.93 us
    pallas_call x1, Pallas kernels, near_field(): pl.pallas_call(functools.partial(near_kernel, first, last), out_shape=jax...  4.89 us
    optimization_barrier x1, local copies, waits for them, and re-layouts, on_device(): own, t1 = tie((own, t1))  4.72 us
  transfers between devices with their start and end apart: 6, of which 2 were waited for; matrix products, arithmetic and copies ran while one was open for 6% of the time, Pallas kernels for 25%

profile of v2, /device:TPU:1, one launch (start us, length us, event | category | flops | bytes accessed | tf_op | source)
XLA Modules:
  0.0 82.6 jit_solution(2780340592411733687)
XLA Ops:
  0.0 2.6 %up_pass.1 = (bf16[16,16,128]{2,1,0:T(8,128)(2,1)}, bf16[24,4096]{1,0:T(8,128)(2,1)}) custom-call(s32[1]{0:T(128)} %bitcast.id_ref, bf16[16,4096]{1,0:T(8,128)(2,1)} %rhs_hbm.1, bf16[3,4096]{1,0:T(4,128)(2,1)} %coords_hbm.1, bf16[16,64,256]{2,1,0:T(8,128)(2,1)} %basis_hbm.3, bf16[16,64,64]{2,1,0:T(8,128)(2,1)} %lt_hbm.3, bf16[1,64,64]{2,1,0:T(8,128)(2,1)} %dt_hbm.3), custom_call_target="tpu_custom_call" | custom-call | flops 20000000 | bytes 1000000 | tf_op jit(solution)/shard_map/up_pass/pallas_call | solution.py:88
  2.6 15.8 %all-to-all-start = ((bf16[16,16,128]{2,1,0:T(8,128)(2,1)}), bf16[16,16,128]{2,1,0:T(8,128)(2,1)S(1)}, u32[]{:S(2)}, u32[]{:S(2)}) async-start(bf16[16,16,128]{2,1,0:T(8,128)(2,1)} %get-tuple-element.25), calls=%async_computation | async-start | bytes 131072 | tf_op jit(solution)/shard_map/all_to_all | solution.py:484
  18.3 3.2 %collective-permute-start = (bf16[24,4096]{1,0:T(8,128)(2,1)}, bf16[24,4096]{1,0:T(8,128)(2,1)S(1)}, u32[]{:S(2)}, u32[]{:S(2)}) collective-permute-start(bf16[24,4096]{1,0:T(8,128)(2,1)} %get-tuple-element.30.own_ref), channel_id=1, source_target_pairs={{0,1},{1,0},{2,3},{3,2},{4,5},{5,4},{6,7},{7,6},{8,9},{9,8},{10,11... | collective-permute-start | bytes 589832 | tf_op jit(solution)/shard_map/ppermute | solution.py:485
  21.6 4.9 %collective-permute-start.1 = (bf16[24,4096]{1,0:T(8,128)(2,1)}, bf16[24,4096]{1,0:T(8,128)(2,1)S(1)}, u32[]{:S(2)}, u32[]{:S(2)}) collective-permute-start(bf16[24,4096]{1,0:T(8,128)(2,1)} %get-tuple-element.30.own_ref), channel_id=1, source_target_pairs={{1,2},{2,1},{3,4},{4,3},{5,6},{6,5},{7,8},{8,7},{9,10},{10,9},{11,... | collective-permute-start | bytes 589832 | tf_op jit(solution)/shard_map/ppermute | solution.py:486
  26.5 4.7 %copy.15.t1_hbm = bf16[128,64,64]{2,1,0:T(8,128)(2,1)} copy(bf16[128,64,64]{0,2,1:T(8,128)(2,1)} %param.19) | data formatting | bytes 2097152 | tf_op jit(solution)/shard_map/optimization_barrier | solution.py:487
  31.2 1.6 %pick_pass.1.one_hbm = bf16[1,64,64]{2,1,0:T(8,128)(2,1)} custom-call(s32[1]{0:T(128)} %bitcast.id_ref, bf16[128,64,64]{2,1,0:T(8,128)(2,1)} %copy.15.t1_hbm), custom_call_target="tpu_custom_call" | custom-call | bytes 32000 | tf_op jit(solution)/shard_map/pick_pass/pallas_call | solution.py:136
  32.8 0.0 collective-permute-done.swap_a_ref
  32.8 0.0 copy-start.4
  32.8 0.0 collective-permute-done.1.swap_b_ref
  32.9 0.0 copy-start.5
  32.9 0.0 all-to-all-done
  32.9 1.2 %broadcast_in_dim.2 = bf16[16,256,128]{2,1,0:T(8,128)(2,1)} broadcast(bf16[256,128]{1,0:T(8,128)(2,1)S(1)} %bitcast.7), dimensions={1,2} | broadcast | bytes 1114112 | tf_op jit(solution)/shard_map/broadcast_in_dim | solution.py:473
  34.1 6.0 %all-to-all-start.1 = ((bf16[16,256,128]{2,1,0:T(8,128)(2,1)}), bf16[16,256,128]{2,1,0:T(8,128)(2,1)S(1)}, u32[]{:S(2)}, u32[]{:S(2)}) async-start(bf16[16,256,128]{2,1,0:T(8,128)(2,1)} %broadcast_in_dim.2), calls=%async_computation.1 | async-start | bytes 2097152 | tf_op jit(solution)/shard_map/all_to_all | solution.py:474
  40.0 0.0 copy-done.4
  40.0 0.0 copy-done.5
  40.1 12.5 %near_and_prep.1 = (f32[16,3072]{1,0:T(8,128)}, bf16[98304,128]{1,0:T(8,128)(2,1)}, bf16[2,64,64]{2,1,0:T(8,128)(2,1)}) custom-call(s32[1]{0:T(128)} %bitcast.id_ref, s32[8,16]{1,0:T(8,128)} %bitcast.8, bf16[24,4096]{1,0:T(8,128)(2,1)} %copy-done.4, bf16[24,4096]{1,0:T(8,128)(2,1)} %get-tuple-element.30.own_ref, bf16[24,4096]{1,0:T(8,128)(2,1)} %copy-done.5, ...), custom_call_target="tpu_custom_call" | custom-call | flops 5600000000 | bytes 600000 | tf_op jit(solution)/shard_map/near_and_prep/pallas_call | solution.py:245
  52.6 2.7 %all-to-all-done.1 = bf16[16,256,128]{2,1,0:T(8,128)(2,1)S(1)} async-done(((bf16[16,256,128]{2,1,0:T(8,128)(2,1)}), bf16[16,256,128]{2,1,0:T(8,128)(2,1)S(1)}, u32[]{:S(2)}, u32[]{:S(2)}) %all-to-all-start.1) | async-done | bytes 1048608 | tf_op jit(solution)/shard_map/all_to_all | solution.py:474
  55.3 5.1 %collective-permute-start.2 = (bf16[4096,128]{1,0:T(8,128)(2,1)S(1)}, bf16[4096,128]{1,0:T(8,128)(2,1)S(1)}, u32[]{:S(2)}, u32[]{:S(2)}) collective-permute-start(bf16[4096,128]{1,0:T(8,128)(2,1)S(1)} %bitcast.4), channel_id=1, source_target_pairs={{0,4},{4,0},{1,5},{5,1},{2,6},{6,2},{3,7},{7,3},{8,12},{12,8},{9,1... | collective-permute-start | bytes 3145736 | tf_op jit(solution)/shard_map/ppermute | solution.py:468
  61.0 0.0 copy-start.1
  61.0 0.0 copy-start.2
  61.0 1.8 %half_pass.1 = (f32[1024,128]{1,0:T(8,128)S(1)}, bf16[10240,128]{1,0:T(8,128)(2,1)S(1)}) custom-call(bf16[4096,128]{1,0:T(8,128)(2,1)S(1)} %bitcast.5, bf16[98304,128]{1,0:T(8,128)(2,1)} %get-tuple-element.35.packed_hbm), custom_call_target="tpu_custom_call" | custom-call | flops 1000000 | bytes 5000000 | tf_op jit(solution)/shard_map/half_pass/pallas_call | solution.py:293
  62.8 0.0 collective-permute-done.2.other_ref
  62.8 0.0 copy-done.1
  62.8 0.0 copy-done.2
  62.8 3.2 %mid_pass.1 = (f32[32,64]{1,0:T(8,128)S(1)}, f32[8,32,128]{2,1,0:T(8,128)}) custom-call(s32[1]{0:T(128)} %bitcast.id_ref, s32[1,16]{1,0:T(1,128)S(1)} %copy-done.2, s32[1]{0:T(128)S(6)} %copy.17.fcount_ref, s32[1,4,8]{2,1,0:T(4,128)S(1)} %copy-done.1, bf16[4096,128]{1,0:T(8,128)(2,1)S(1)} %bitcast.6, bf16[4096,128]{1,0:T(8,128)(2,1)S(1)} %collective-permute-done.2.other_ref, ...), custom_call_target="tpu_custom_call" | custom-call | flops 300000000 | bytes 5000000 | tf_op jit(solution)/shard_map/mid_pass/pallas_call | solution.py:390
  66.0 0.0 copy-start
  66.0 0.6 copy-done
  66.6 6.8 %all-to-all-start.2 = ((f32[8,32,128]{2,1,0:T(8,128)}), f32[8,32,128]{2,1,0:T(8,128)S(1)}, u32[]{:S(2)}, u32[]{:S(2)}) async-start(f32[8,32,128]{2,1,0:T(8,128)} %get-tuple-element.40), calls=%async_computation.2 | async-start | bytes 262144 | tf_op jit(solution)/shard_map/all_to_all | solution.py:501
  73.4 4.9 %near_field.1.near_b_hbm = f32[16,1024]{1,0:T(8,128)} custom-call(s32[1]{0:T(128)} %bitcast.id_ref, s32[8,16]{1,0:T(8,128)} %bitcast.9, bf16[24,4096]{1,0:T(8,128)(2,1)} %copy-done.4, bf16[24,4096]{1,0:T(8,128)(2,1)} %get-tuple-element.30.own_ref, bf16[24,4096]{1,0:T(8,128)(2,1)} %copy-done.5), custom_call_target="tpu_custom_call" | custom-call | flops 2000000000 | bytes 600000 | tf_op jit(solution)/shard_map/near_field/pallas_call | solution.py:271
  78.3 0.9 %all-to-all-done.2.shares_hbm = f32[8,32,128]{2,1,0:T(8,128)S(1)} async-done(((f32[8,32,128]{2,1,0:T(8,128)}), f32[8,32,128]{2,1,0:T(8,128)S(1)}, u32[]{:S(2)}, u32[]{:S(2)}) %all-to-all-start.2) | async-done | bytes 131104 | tf_op jit(solution)/shard_map/all_to_all | solution.py:501
  79.2 0.0 copy-start.3
  79.2 0.7 copy-done.3
  79.9 2.7 %down_pass.1 = f32[16,4096]{1,0:T(8,128)} custom-call(s32[1]{0:T(128)} %bitcast.id_ref, f32[32,64]{1,0:T(8,128)} %copy-done, f32[8,32,128]{2,1,0:T(8,128)} %copy-done.3, bf16[2,64,64]{2,1,0:T(8,128)(2,1)} %get-tuple-element.41.path_hbm, bf16[1,64,64]{2,1,0:T(8,128)(2,1)} %pick_pass.1.one_hbm, bf16[1,64,64]{2,1,0:T(8,128)(2,1)} %dt_hbm.3, ...), custom_call_target="tpu_custom_call" | custom-call | flops 20000000 | bytes 1500000 | tf_op jit(solution)/shard_map/down_pass/pallas_call | solution.py:444
Async XLA Ops:
  2.6 30.3 %all-to-all-start = ((bf16[16,16,128]{2,1,0:T(8,128)(2,1)}), bf16[16,16,128]{2,1,0:T(8,128)(2,1)S(1)}, u32[]{:S(2)}, u32[]{:S(2)}) async-start(bf16[16,16,128]{2,1,0:T(8,128)(2,1)} %get-tuple-element.25), calls=%async_computation | async-start | bytes 131072 | tf_op jit(solution)/shard_map/all_to_all | solution.py:484
  18.3 14.5 %collective-permute-start = (bf16[24,4096]{1,0:T(8,128)(2,1)}, bf16[24,4096]{1,0:T(8,128)(2,1)S(1)}, u32[]{:S(2)}, u32[]{:S(2)}) collective-permute-start(bf16[24,4096]{1,0:T(8,128)(2,1)} %get-tuple-element.30.own_ref), channel_id=1, source_target_pairs={{0,1},{1,0},{2,3},{3,2},{4,5},{5,4},{6,7},{7,6},{8,9},{9,8},{10,11... | collective-permute-start | bytes 589832 | tf_op jit(solution)/shard_map/ppermute | solution.py:485
  21.6 11.3 %collective-permute-start.1 = (bf16[24,4096]{1,0:T(8,128)(2,1)}, bf16[24,4096]{1,0:T(8,128)(2,1)S(1)}, u32[]{:S(2)}, u32[]{:S(2)}) collective-permute-start(bf16[24,4096]{1,0:T(8,128)(2,1)} %get-tuple-element.30.own_ref), channel_id=1, source_target_pairs={{1,2},{2,1},{3,4},{4,3},{5,6},{6,5},{7,8},{8,7},{9,10},{10,9},{11,... | collective-permute-start | bytes 589832 | tf_op jit(solution)/shard_map/ppermute | solution.py:486
  32.8 7.2 %copy-start.4 = (bf16[24,4096]{1,0:T(8,128)(2,1)}, bf16[24,4096]{1,0:T(8,128)(2,1)S(1)}, u32[]{:S(2)}) copy-start(bf16[24,4096]{1,0:T(8,128)(2,1)S(1)} %collective-permute-done.swap_a_ref) | copy-start | bytes 589828
  32.9 7.2 %copy-start.5 = (bf16[24,4096]{1,0:T(8,128)(2,1)}, bf16[24,4096]{1,0:T(8,128)(2,1)S(1)}, u32[]{:S(2)}) copy-start(bf16[24,4096]{1,0:T(8,128)(2,1)S(1)} %collective-permute-done.1.swap_b_ref) | copy-start | bytes 589828
  34.1 21.2 %all-to-all-start.1 = ((bf16[16,256,128]{2,1,0:T(8,128)(2,1)}), bf16[16,256,128]{2,1,0:T(8,128)(2,1)S(1)}, u32[]{:S(2)}, u32[]{:S(2)}) async-start(bf16[16,256,128]{2,1,0:T(8,128)(2,1)} %broadcast_in_dim.2), calls=%async_computation.1 | async-start | bytes 2097152 | tf_op jit(solution)/shard_map/all_to_all | solution.py:474
  55.3 7.6 %collective-permute-start.2 = (bf16[4096,128]{1,0:T(8,128)(2,1)S(1)}, bf16[4096,128]{1,0:T(8,128)(2,1)S(1)}, u32[]{:S(2)}, u32[]{:S(2)}) collective-permute-start(bf16[4096,128]{1,0:T(8,128)(2,1)S(1)} %bitcast.4), channel_id=1, source_target_pairs={{0,4},{4,0},{1,5},{5,1},{2,6},{6,2},{3,7},{7,3},{8,12},{12,8},{9,1... | collective-permute-start | bytes 3145736 | tf_op jit(solution)/shard_map/ppermute | solution.py:468
  61.0 1.8 %copy-start.1 = (s32[1,4,8]{2,1,0:T(4,128)S(1)}, s32[1,4,8]{2,1,0:T(4,128)}, u32[]{:S(2)}) copy-start(s32[1,4,8]{2,1,0:T(4,128)} %tlist_ref.1) | copy-start | bytes 388
  61.0 1.8 %copy-start.2 = (s32[1,16]{1,0:T(1,128)S(1)}, s32[1,16]{1,0:T(1,128)}, u32[]{:S(2)}) copy-start(s32[1,16]{1,0:T(1,128)} %flist_ref.1) | copy-start | bytes 196
  66.0 0.6 copy-start
  66.6 12.6 %all-to-all-start.2 = ((f32[8,32,128]{2,1,0:T(8,128)}), f32[8,32,128]{2,1,0:T(8,128)S(1)}, u32[]{:S(2)}, u32[]{:S(2)}) async-start(f32[8,32,128]{2,1,0:T(8,128)} %get-tuple-element.40), calls=%async_computation.2 | async-start | bytes 262144 | tf_op jit(solution)/shard_map/all_to_all | solution.py:501
  79.2 0.7 copy-start.3

commit v3 on v2

--- a/solution.py
+++ b/solution.py
@@ -122,26 +122,24 @@
         for slot in range(8):
             put(128 + level * 8 + slot, tc_ref[0, level, slot], tc_ref[0, level, slot])
     branch = id_ref[0] >> 2
-    path_ref[0] = t2_ref[branch >> 1]
-    path_ref[1] = t3_ref[branch >> 2]
-
-
-def pick_kernel(id_ref, t1_hbm, out_hbm, sem):
-    move = pltpu.make_async_copy(t1_hbm.at[pl.ds(id_ref[0] >> 2, 1)], out_hbm, sem)
-    move.start()
-    move.wait()
-
-
-def pick_pass(dev, t1):
-    return pl.pallas_call(
-        pick_kernel,
-        out_shape=jax.ShapeDtypeStruct((1, 64, 64), BF16),
+    path_ref[0] = t1_ref[branch]
+    path_ref[1] = t2_ref[branch >> 1]
+    path_ref[2] = t3_ref[branch >> 2]
+
+
+def order_kernel(id_ref, t1_hbm, out_ref):
+    out_ref[0] = id_ref[0]
+
+
+def order_pass(dev, t1):
+    return pl.pallas_call(
+        order_kernel,
+        out_shape=jax.ShapeDtypeStruct((1,), jnp.int32),
         in_specs=smem(1) + hbm(1),
-        out_specs=hbm(1)[0],
-        scratch_shapes=[pltpu.SemaphoreType.DMA],
+        out_specs=smem(1)[0],
         compiler_params=pltpu.CompilerParams(vmem_limit_bytes=GRANT),
-        cost_estimate=pl.CostEstimate(flops=0, bytes_accessed=32_000, transcendentals=0),
-        name="pick_pass",
+        cost_estimate=pl.CostEstimate(flops=0, bytes_accessed=64, transcendentals=0),
+        name="order_pass",
     )(dev, t1)
 
 
@@ -202,7 +200,7 @@
         out_ref[:, pl.ds(pl.multiple_of(step * 256, 256), 256)] = total
         return carry
 
-    lax.fori_loop(0, last - first, leaf_step, 0, unroll=4)
+    lax.fori_loop(0, last - first, leaf_step, 0, unroll=min(6, last - first))
 
 
 def near_and_prep_kernel(
@@ -247,7 +245,7 @@
         out_shape=[
             jax.ShapeDtypeStruct((16, (last - first) * 256), F32),
             jax.ShapeDtypeStruct((ROOM, 128), BF16),
-            jax.ShapeDtypeStruct((2, 64, 64), BF16),
+            jax.ShapeDtypeStruct((3, 64, 64), BF16),
         ],
         in_specs=smem(2) + vmem(3) + hbm(5),
         out_specs=vmem(1) + hbm(1) + vmem(1),
@@ -307,7 +305,7 @@
 
 def mid_kernel(
     id_ref, flist_ref, fcount_ref, tlist_ref, own_ref, other_ref, sums_ref, packed,
-    out_ref, shares_ref, nodes,
+    shares_ref, nodes,
 ):
     my_core = (id_ref[0] >> 2) & 1
     lane16 = lax.broadcasted_iota(jnp.int32, (16, 128), 1)
@@ -366,7 +364,7 @@
         block = jnp.where(c_core == my_core, own_ref[pl.ds(place, 16), :], other_ref[pl.ds(place, 16), :])
         live = jnp.where(slot < fcount_ref[0], 1 - c_core, 2)
         blocks.append(block * jnp.where(half16 == live, 1.0, 0.0).astype(BF16))
-    out_ref[16:32, :] = dot(jnp.concatenate(blocks, axis=1), side_by_side(112, 16), NT)
+    far = dot(jnp.concatenate(blocks, axis=1), side_by_side(112, 16), NT)
 
     parts = []
     for level, offset in enumerate((0, 64, 96, 112)):
@@ -378,23 +376,21 @@
             blocks.append(block * jnp.concatenate([mask, mask], axis=0))
         out = dot(jnp.concatenate(blocks, axis=1), side_by_side(128 + level * 8, 8), NT)
         parts.append(out[:16] + out[16:])
-    out_ref[0:16, :] = parts[0]
     upper = jnp.concatenate([parts[1], parts[2]], axis=1)
-    last = jnp.concatenate([parts[3], parts[3]], axis=1)
+    last = jnp.concatenate([parts[3], parts[0]], axis=1)
+    far = jnp.concatenate([far, far], axis=1)
     for k in range(8):
         shares_ref[k, 0:16, :] = upper
         shares_ref[k, 16:32, :] = last
+        shares_ref[k, 32:48, :] = far
 
 
 def mid_pass(dev, flist, fcount, tlist, own, other, sums, packed):
     return pl.pallas_call(
         mid_kernel,
-        out_shape=[
-            jax.ShapeDtypeStruct((32, 64), F32),
-            jax.ShapeDtypeStruct((8, 32, 128), F32),
-        ],
+        out_shape=jax.ShapeDtypeStruct((8, 48, 128), F32),
         in_specs=smem(4) + vmem(4),
-        out_specs=vmem(2),
+        out_specs=vmem(1)[0],
         scratch_shapes=[pltpu.VMEM((120, 32, 128), BF16)],
         compiler_params=pltpu.CompilerParams(vmem_limit_bytes=GRANT - 16 * 1024 * 1024),
         cost_estimate=pl.CostEstimate(flops=300_000_000, bytes_accessed=5_000_000, transcendentals=0),
@@ -403,19 +399,20 @@
 
 
 def down_kernel(
-    id_ref, mid_hbm, shares_hbm, path_hbm, one_hbm, dt_hbm, lt_hbm, basis_hbm, near_a_hbm, near_b_hbm,
-    out_ref, mid_ref, shares_ref, path_ref, one_ref, dt_ref, lt_ref, basis_ref, near_a, near_b, sems,
+    id_ref, shares_hbm, path_hbm, dt_hbm, lt_hbm, basis_hbm, near_a_hbm, near_b_hbm,
+    out_ref, shares_ref, path_ref, dt_ref, lt_ref, basis_ref, near_a, near_b, sems,
 ):
     moves = copies(
-        (mid_hbm, shares_hbm, path_hbm, one_hbm, dt_hbm, lt_hbm, basis_hbm, near_a_hbm, near_b_hbm),
-        (mid_ref, shares_ref, path_ref, one_ref, dt_ref, lt_ref, basis_ref, near_a, near_b),
+        (shares_hbm, path_hbm, dt_hbm, lt_hbm, basis_hbm, near_a_hbm, near_b_hbm),
+        (shares_ref, path_ref, dt_ref, lt_ref, basis_ref, near_a, near_b),
         sems,
     )
     for move in moves:
         move.start()
-    for move in moves[:5]:
+    for move in moves[:3]:
         move.wait()
     zl = (id_ref[0] >> 3) & 3
+    mine = shares_ref[(id_ref[0] >> 2) & 7]
     upper = jnp.zeros((16, 128), F32)
     down = jnp.zeros((16, 64), F32)
     low = lax.broadcasted_iota(jnp.int32, (16, 128), 1) < 64
@@ -424,11 +421,11 @@
         quad = jnp.where((o >> 2) == (zl >> 1), 1.0, 0.0)
         upper = upper + shares_ref[o, 0:16, :] * jnp.where(low, pair, quad)
         down = down + shares_ref[o, 16:32, 0:64]
-    down = upper[:, 64:128] + wide_dot(down, path_ref[1], NN)
-    down = upper[:, 0:64] + wide_dot(down, path_ref[0], NN)
-    down = mid_ref[0:16, :] + wide_dot(down, one_ref[0], NN)
-    down = mid_ref[16:32, :] + wide_dot(down, dt_ref[0], NN)
-    for move in moves[5:]:
+    down = upper[:, 64:128] + wide_dot(down, path_ref[2], NN)
+    down = upper[:, 0:64] + wide_dot(down, path_ref[1], NN)
+    down = mine[16:32, 64:128] + wide_dot(down, path_ref[0], NN)
+    down = mine[32:48, 0:64] + wide_dot(down, dt_ref[0], NN)
+    for move in moves[3:]:
         move.wait()
     near_refs = (near_a, near_b)
     near_blocks = [(ref, k) for ref in near_refs for k in range(ref.shape[1] // 256)]
@@ -440,28 +437,26 @@
         out_ref[:, cols] = near + dot(leaf_down, basis_ref[leaf], NN)
 
 
-def down_pass(dev, mid, shares, path, one, dt, lt, basis, near):
+def down_pass(dev, shares, path, dt, lt, basis, near):
     return pl.pallas_call(
         down_kernel,
         out_shape=jax.ShapeDtypeStruct((16, 4096), F32),
-        in_specs=smem(1) + hbm(9),
+        in_specs=smem(1) + hbm(7),
         out_specs=vmem(1)[0],
         scratch_shapes=[
-            pltpu.VMEM((32, 64), F32),
-            pltpu.VMEM((8, 32, 128), F32),
-            pltpu.VMEM((2, 64, 64), BF16),
-            pltpu.VMEM((1, 64, 64), BF16),
+            pltpu.VMEM((8, 48, 128), F32),
+            pltpu.VMEM((3, 64, 64), BF16),
             pltpu.VMEM((1, 64, 64), BF16),
             pltpu.VMEM((16, 64, 64), BF16),
             pltpu.VMEM((16, 64, 256), BF16),
             pltpu.VMEM(near[0].shape, F32),
             pltpu.VMEM(near[1].shape, F32),
-            pltpu.SemaphoreType.DMA((9,)),
+            pltpu.SemaphoreType.DMA((7,)),
         ],
         compiler_params=pltpu.CompilerParams(vmem_limit_bytes=GRANT),
         cost_estimate=pl.CostEstimate(flops=20_000_000, bytes_accessed=1_500_000, transcendentals=0),
         name="down_pass",
-    )(dev, mid, shares, path, one, dt, lt, basis, *near)
+    )(dev, shares, path, dt, lt, basis, *near)
 
 
 def cyclic(value, axis, size, by):
@@ -485,21 +480,21 @@
     swap_a = lax.ppermute(own, DEV, [(i, i ^ 1) for i in range(512)])
     swap_b = lax.ppermute(own, DEV, [(i, ((i + 1) ^ 1) - 1) for i in range(1, 511)] + [(0, 511), (511, 0)])
     own, t1 = tie((own, t1))
-    one = pick_pass(dev, t1)
-    blocks, swap_a, swap_b, one = tie((blocks, swap_a, swap_b, one))
+    dev_a = order_pass(dev, t1)
+    blocks, swap_a, swap_b, dev_a = tie((blocks, swap_a, swap_b, dev_a))
     near_list = jnp.transpose(near_list)
     gathered = spread(blocks, ("x", "y"), 16)
     near_a, packed, path = near_and_prep(
-        dev, near_list, swap_a, own, swap_b, t1, t2, t3, far_coupling, top_coupling, 0, 12
+        dev_a, near_list, swap_a, own, swap_b, t1, t2, t3, far_coupling, top_coupling, 0, 12
     )
     gathered, near_a, packed = tie((gathered, near_a, packed))
     other = cyclic(gathered, "core", 2, 1)
     sums, packed = half_pass(gathered, packed)
-    mid, shares = mid_pass(dev, far_list, far_count, top_list, gathered, other, sums, packed)
+    shares = mid_pass(dev, far_list, far_count, top_list, gathered, other, sums, packed)
     shares, dev_b = tie((shares, dev))
     near_b = near_field(dev_b, near_list, swap_a, own, swap_b, 12, 16)
     shares = lax.all_to_all(shares, ("zl", "core"), 0, 0, tiled=True)
-    return down_pass(dev, mid, shares, path, one, dt, lt, basis, (near_a, near_b))
+    return down_pass(dev, shares, path, dt, lt, basis, (near_a, near_b))
 
 
 def solution(mesh):

time: 83.2 us -> 81.8 us (0.983)
    pallas_call x2, Pallas kernels: 4.76 us -> 3.61 us  [the longest x1 3.1 us: mid_pass(): pl.pallas_call(mid_kernel, out_shape=jax.ShapeDtypeStruct((8, 48, 128), F...]
where the time goes in v3:
time: 81.8 us; the launch traced here: 81.2 us
  starting transfers between devices  41.2 us (50%)
  Pallas kernels  28.6 us (35%)
  local copies, waits for them, and re-layouts  6.58 us (8%)
  waiting for transfers between devices  3.83 us (5%)
  between operations  0.98 us (1%)
    all_to_all x1, starting transfers between devices, on_device(): lax.all_to_all(payload, ('zh', 'zl'), 0, 0, tiled=True).reshape(256, 128)  15.8 us
    pallas_call x1, Pallas kernels, near_and_prep(): pl.pallas_call(functools.partial(near_and_prep_kernel, first, last), out_...  12.9 us
    all_to_all x1, starting transfers between devices, on_device(): shares = lax.all_to_all(shares, ('zl', 'core'), 0, 0, tiled=True)  6.37 us
    all_to_all x1, starting transfers between devices, spread(): lax.all_to_all(same, axis, 0, 0, tiled=True).reshape(size * rows, 128)  5.97 us
    ppermute x1, starting transfers between devices, cyclic(): lax.ppermute(value, axis, [(i, (i + by) % size) for i in range(size)])  4.99 us
    ppermute x1, starting transfers between devices, on_device(): lax.ppermute(own, DEV, [(i, (i + 1 ^ 1) - 1) for i in range(1, 511)] + [(...  4.93 us
    pallas_call x1, Pallas kernels, near_field(): pl.pallas_call(functools.partial(near_kernel, first, last), out_shape=jax...  4.88 us
    optimization_barrier x1, local copies, waits for them, and re-layouts, on_device(): own, t1 = tie((own, t1))  4.7 us
  transfers between devices with their start and end apart: 6, of which 2 were waited for; matrix products, arithmetic and copies ran while one was open for 6% of the time, Pallas kernels for 25%

profile of v3, /device:TPU:1, one launch (start us, length us, event | category | flops | bytes accessed | tf_op | source)
XLA Modules:
  0.0 81.2 jit_solution(5605500897252250857)
XLA Ops:
  0.0 2.6 %up_pass.1 = (bf16[16,16,128]{2,1,0:T(8,128)(2,1)}, bf16[24,4096]{1,0:T(8,128)(2,1)}) custom-call(s32[1]{0:T(128)} %bitcast.id_ref, bf16[16,4096]{1,0:T(8,128)(2,1)} %rhs_hbm.1, bf16[3,4096]{1,0:T(4,128)(2,1)} %coords_hbm.1, bf16[16,64,256]{2,1,0:T(8,128)(2,1)} %basis_hbm.3, bf16[16,64,64]{2,1,0:T(8,128)(2,1)} %lt_hbm.3, bf16[1,64,64]{2,1,0:T(8,128)(2,1)} %dt_hbm.3), custom_call_target="tpu_custom_call" | custom-call | flops 20000000 | bytes 1000000 | tf_op jit(solution)/shard_map/up_pass/pallas_call | solution.py:88
  2.6 15.8 %all-to-all-start = ((bf16[16,16,128]{2,1,0:T(8,128)(2,1)}), bf16[16,16,128]{2,1,0:T(8,128)(2,1)S(1)}, u32[]{:S(2)}, u32[]{:S(2)}) async-start(bf16[16,16,128]{2,1,0:T(8,128)(2,1)} %get-tuple-element.23), calls=%async_computation | async-start | bytes 131072 | tf_op jit(solution)/shard_map/all_to_all | solution.py:479
  18.3 3.2 %collective-permute-start = (bf16[24,4096]{1,0:T(8,128)(2,1)}, bf16[24,4096]{1,0:T(8,128)(2,1)S(1)}, u32[]{:S(2)}, u32[]{:S(2)}) collective-permute-start(bf16[24,4096]{1,0:T(8,128)(2,1)} %get-tuple-element.29.own_ref), channel_id=1, source_target_pairs={{0,1},{1,0},{2,3},{3,2},{4,5},{5,4},{6,7},{7,6},{8,9},{9,8},{10,11... | collective-permute-start | bytes 589832 | tf_op jit(solution)/shard_map/ppermute | solution.py:480
  21.6 4.9 %collective-permute-start.1 = (bf16[24,4096]{1,0:T(8,128)(2,1)}, bf16[24,4096]{1,0:T(8,128)(2,1)S(1)}, u32[]{:S(2)}, u32[]{:S(2)}) collective-permute-start(bf16[24,4096]{1,0:T(8,128)(2,1)} %get-tuple-element.29.own_ref), channel_id=1, source_target_pairs={{1,2},{2,1},{3,4},{4,3},{5,6},{6,5},{7,8},{8,7},{9,10},{10,9},{11,... | collective-permute-start | bytes 589832 | tf_op jit(solution)/shard_map/ppermute | solution.py:481
  26.5 4.7 %copy.15.t1_hbm = bf16[128,64,64]{2,1,0:T(8,128)(2,1)} copy(bf16[128,64,64]{0,2,1:T(8,128)(2,1)} %param.19) | data formatting | bytes 2097152 | tf_op jit(solution)/shard_map/optimization_barrier | solution.py:482
  31.2 0.5 order_pass.1.id_ref
  31.7 0.0 collective-permute-done.swap_a_ref
  31.7 0.0 copy-start.3
  31.7 0.0 collective-permute-done.1.swap_b_ref
  31.7 0.0 copy-start.4
  31.8 0.0 all-to-all-done
  31.8 1.2 %broadcast_in_dim.2 = bf16[16,256,128]{2,1,0:T(8,128)(2,1)} broadcast(bf16[256,128]{1,0:T(8,128)(2,1)S(1)} %bitcast.7), dimensions={1,2} | broadcast | bytes 1114112 | tf_op jit(solution)/shard_map/broadcast_in_dim | solution.py:468
  32.9 6.0 %all-to-all-start.1 = ((bf16[16,256,128]{2,1,0:T(8,128)(2,1)}), bf16[16,256,128]{2,1,0:T(8,128)(2,1)S(1)}, u32[]{:S(2)}, u32[]{:S(2)}) async-start(bf16[16,256,128]{2,1,0:T(8,128)(2,1)} %broadcast_in_dim.2), calls=%async_computation.1 | async-start | bytes 2097152 | tf_op jit(solution)/shard_map/all_to_all | solution.py:469
  38.9 0.0 copy-done.3
  38.9 0.0 copy-done.4
  38.9 12.9 %near_and_prep.1 = (f32[16,3072]{1,0:T(8,128)}, bf16[98304,128]{1,0:T(8,128)(2,1)}, bf16[3,64,64]{2,1,0:T(8,128)(2,1)}) custom-call(s32[1]{0:T(128)} %order_pass.1.id_ref, s32[8,16]{1,0:T(8,128)} %bitcast.8, bf16[24,4096]{1,0:T(8,128)(2,1)} %copy-done.3, bf16[24,4096]{1,0:T(8,128)(2,1)} %get-tuple-element.29.own_ref, bf16[24,4096]{1,0:T(8,128)(2,1)} %copy-done.4, ...), custom_call_target="tpu_custom_call" | custom-call | flops 5600000000 | bytes 600000 | tf_op jit(solution)/shard_map/near_and_prep/pallas_call | solution.py:243
  51.9 2.2 %all-to-all-done.1 = bf16[16,256,128]{2,1,0:T(8,128)(2,1)S(1)} async-done(((bf16[16,256,128]{2,1,0:T(8,128)(2,1)}), bf16[16,256,128]{2,1,0:T(8,128)(2,1)S(1)}, u32[]{:S(2)}, u32[]{:S(2)}) %all-to-all-start.1) | async-done | bytes 1048608 | tf_op jit(solution)/shard_map/all_to_all | solution.py:469
  54.1 5.0 %collective-permute-start.2 = (bf16[4096,128]{1,0:T(8,128)(2,1)S(1)}, bf16[4096,128]{1,0:T(8,128)(2,1)S(1)}, u32[]{:S(2)}, u32[]{:S(2)}) collective-permute-start(bf16[4096,128]{1,0:T(8,128)(2,1)S(1)} %bitcast.4), channel_id=1, source_target_pairs={{0,4},{4,0},{1,5},{5,1},{2,6},{6,2},{3,7},{7,3},{8,12},{12,8},{9,1... | collective-permute-start | bytes 3145736 | tf_op jit(solution)/shard_map/ppermute | solution.py:463
  59.8 0.0 copy-start
  59.8 0.0 copy-start.1
  59.8 1.8 %half_pass.1 = (f32[1024,128]{1,0:T(8,128)S(1)}, bf16[10240,128]{1,0:T(8,128)(2,1)S(1)}) custom-call(bf16[4096,128]{1,0:T(8,128)(2,1)S(1)} %bitcast.5, bf16[98304,128]{1,0:T(8,128)(2,1)} %get-tuple-element.34.packed_hbm), custom_call_target="tpu_custom_call" | custom-call | flops 1000000 | bytes 5000000 | tf_op jit(solution)/shard_map/half_pass/pallas_call | solution.py:291
  61.5 0.0 collective-permute-done.2.other_ref
  61.6 0.0 copy-done
  61.6 0.0 copy-done.1
  61.6 3.1 %mid_pass.1 = f32[8,48,128]{2,1,0:T(8,128)} custom-call(s32[1]{0:T(128)} %bitcast.id_ref, s32[1,16]{1,0:T(1,128)S(1)} %copy-done.1, s32[1]{0:T(128)S(6)} %copy.17.fcount_ref, s32[1,4,8]{2,1,0:T(4,128)S(1)} %copy-done, bf16[4096,128]{1,0:T(8,128)(2,1)S(1)} %bitcast.6, bf16[4096,128]{1,0:T(8,128)(2,1)S(1)} %collective-permute-done.2.other_ref, ...), custom_call_target="tpu_custom_call" | custom-call | flops 300000000 | bytes 5000000 | tf_op jit(solution)/shard_map/mid_pass/pallas_call | solution.py:389
  64.7 6.4 %all-to-all-start.2 = ((f32[8,48,128]{2,1,0:T(8,128)}), f32[8,48,128]{2,1,0:T(8,128)S(1)}, u32[]{:S(2)}, u32[]{:S(2)}) async-start(f32[8,48,128]{2,1,0:T(8,128)} %mid_pass.1), calls=%async_computation.2 | async-start | bytes 393216 | tf_op jit(solution)/shard_map/all_to_all | solution.py:496
  71.0 4.9 %near_field.1.near_b_hbm = f32[16,1024]{1,0:T(8,128)} custom-call(s32[1]{0:T(128)} %bitcast.id_ref, s32[8,16]{1,0:T(8,128)} %bitcast.9, bf16[24,4096]{1,0:T(8,128)(2,1)} %copy-done.3, bf16[24,4096]{1,0:T(8,128)(2,1)} %get-tuple-element.29.own_ref, bf16[24,4096]{1,0:T(8,128)(2,1)} %copy-done.4), custom_call_target="tpu_custom_call" | custom-call | flops 2000000000 | bytes 600000 | tf_op jit(solution)/shard_map/near_field/pallas_call | solution.py:269
  75.9 1.6 %all-to-all-done.2.shares_hbm = f32[8,48,128]{2,1,0:T(8,128)S(1)} async-done(((f32[8,48,128]{2,1,0:T(8,128)}), f32[8,48,128]{2,1,0:T(8,128)S(1)}, u32[]{:S(2)}, u32[]{:S(2)}) %all-to-all-start.2) | async-done | bytes 196640 | tf_op jit(solution)/shard_map/all_to_all | solution.py:496
  77.5 0.0 copy-start.2
  77.5 0.7 copy-done.2
  78.2 2.8 %down_pass.1 = f32[16,4096]{1,0:T(8,128)} custom-call(s32[1]{0:T(128)} %bitcast.id_ref, f32[8,48,128]{2,1,0:T(8,128)} %copy-done.2, bf16[3,64,64]{2,1,0:T(8,128)(2,1)} %get-tuple-element.38.path_hbm, bf16[1,64,64]{2,1,0:T(8,128)(2,1)} %dt_hbm.3, bf16[16,64,64]{2,1,0:T(8,128)(2,1)} %lt_hbm.3, bf16[16,64,256]{2,1,0:T(8,128)(2,1)} %basis_hbm.3, ...), custom_call_target="tpu_custom_call" | custom-call | flops 20000000 | bytes 1500000 | tf_op jit(solution)/shard_map/down_pass/pallas_call | solution.py:441
Async XLA Ops:
  2.6 29.2 %all-to-all-start = ((bf16[16,16,128]{2,1,0:T(8,128)(2,1)}), bf16[16,16,128]{2,1,0:T(8,128)(2,1)S(1)}, u32[]{:S(2)}, u32[]{:S(2)}) async-start(bf16[16,16,128]{2,1,0:T(8,128)(2,1)} %get-tuple-element.23), calls=%async_computation | async-start | bytes 131072 | tf_op jit(solution)/shard_map/all_to_all | solution.py:479
  18.3 13.4 %collective-permute-start = (bf16[24,4096]{1,0:T(8,128)(2,1)}, bf16[24,4096]{1,0:T(8,128)(2,1)S(1)}, u32[]{:S(2)}, u32[]{:S(2)}) collective-permute-start(bf16[24,4096]{1,0:T(8,128)(2,1)} %get-tuple-element.29.own_ref), channel_id=1, source_target_pairs={{0,1},{1,0},{2,3},{3,2},{4,5},{5,4},{6,7},{7,6},{8,9},{9,8},{10,11... | collective-permute-start | bytes 589832 | tf_op jit(solution)/shard_map/ppermute | solution.py:480
  21.6 10.2 %collective-permute-start.1 = (bf16[24,4096]{1,0:T(8,128)(2,1)}, bf16[24,4096]{1,0:T(8,128)(2,1)S(1)}, u32[]{:S(2)}, u32[]{:S(2)}) collective-permute-start(bf16[24,4096]{1,0:T(8,128)(2,1)} %get-tuple-element.29.own_ref), channel_id=1, source_target_pairs={{1,2},{2,1},{3,4},{4,3},{5,6},{6,5},{7,8},{8,7},{9,10},{10,9},{11,... | collective-permute-start | bytes 589832 | tf_op jit(solution)/shard_map/ppermute | solution.py:481
  31.7 7.2 %copy-start.3 = (bf16[24,4096]{1,0:T(8,128)(2,1)}, bf16[24,4096]{1,0:T(8,128)(2,1)S(1)}, u32[]{:S(2)}) copy-start(bf16[24,4096]{1,0:T(8,128)(2,1)S(1)} %collective-permute-done.swap_a_ref) | copy-start | bytes 589828
  31.7 7.2 %copy-start.4 = (bf16[24,4096]{1,0:T(8,128)(2,1)}, bf16[24,4096]{1,0:T(8,128)(2,1)S(1)}, u32[]{:S(2)}) copy-start(bf16[24,4096]{1,0:T(8,128)(2,1)S(1)} %collective-permute-done.1.swap_b_ref) | copy-start | bytes 589828
  32.9 21.2 %all-to-all-start.1 = ((bf16[16,256,128]{2,1,0:T(8,128)(2,1)}), bf16[16,256,128]{2,1,0:T(8,128)(2,1)S(1)}, u32[]{:S(2)}, u32[]{:S(2)}) async-start(bf16[16,256,128]{2,1,0:T(8,128)(2,1)} %broadcast_in_dim.2), calls=%async_computation.1 | async-start | bytes 2097152 | tf_op jit(solution)/shard_map/all_to_all | solution.py:469
  54.1 7.4 %collective-permute-start.2 = (bf16[4096,128]{1,0:T(8,128)(2,1)S(1)}, bf16[4096,128]{1,0:T(8,128)(2,1)S(1)}, u32[]{:S(2)}, u32[]{:S(2)}) collective-permute-start(bf16[4096,128]{1,0:T(8,128)(2,1)S(1)} %bitcast.4), channel_id=1, source_target_pairs={{0,4},{4,0},{1,5},{5,1},{2,6},{6,2},{3,7},{7,3},{8,12},{12,8},{9,1... | collective-permute-start | bytes 3145736 | tf_op jit(solution)/shard_map/ppermute | solution.py:463
  59.8 1.8 %copy-start = (s32[1,4,8]{2,1,0:T(4,128)S(1)}, s32[1,4,8]{2,1,0:T(4,128)}, u32[]{:S(2)}) copy-start(s32[1,4,8]{2,1,0:T(4,128)} %tlist_ref.1) | copy-start | bytes 388
  59.8 1.8 %copy-start.1 = (s32[1,16]{1,0:T(1,128)S(1)}, s32[1,16]{1,0:T(1,128)}, u32[]{:S(2)}) copy-start(s32[1,16]{1,0:T(1,128)} %flist_ref.1) | copy-start | bytes 196
  64.7 12.8 %all-to-all-start.2 = ((f32[8,48,128]{2,1,0:T(8,128)}), f32[8,48,128]{2,1,0:T(8,128)S(1)}, u32[]{:S(2)}, u32[]{:S(2)}) async-start(f32[8,48,128]{2,1,0:T(8,128)} %mid_pass.1), calls=%async_computation.2 | async-start | bytes 393216 | tf_op jit(solution)/shard_map/all_to_all | solution.py:496
  77.5 0.7 copy-start.2

commit v4 on v3

--- a/solution.py
+++ b/solution.py
@@ -200,7 +200,7 @@
         out_ref[:, pl.ds(pl.multiple_of(step * 256, 256), 256)] = total
         return carry
 
-    lax.fori_loop(0, last - first, leaf_step, 0, unroll=min(6, last - first))
+    lax.fori_loop(0, last - first, leaf_step, 0, unroll=4)
 
 
 def near_and_prep_kernel(
@@ -379,16 +379,15 @@
     upper = jnp.concatenate([parts[1], parts[2]], axis=1)
     last = jnp.concatenate([parts[3], parts[0]], axis=1)
     far = jnp.concatenate([far, far], axis=1)
+    packed_shares = jnp.concatenate([upper, last, far], axis=0).astype(BF16)
     for k in range(8):
-        shares_ref[k, 0:16, :] = upper
-        shares_ref[k, 16:32, :] = last
-        shares_ref[k, 32:48, :] = far
+        shares_ref[k] = packed_shares
 
 
 def mid_pass(dev, flist, fcount, tlist, own, other, sums, packed):
     return pl.pallas_call(
         mid_kernel,
-        out_shape=jax.ShapeDtypeStruct((8, 48, 128), F32),
+        out_shape=jax.ShapeDtypeStruct((8, 48, 128), BF16),
         in_specs=smem(4) + vmem(4),
         out_specs=vmem(1)[0],
         scratch_shapes=[pltpu.VMEM((120, 32, 128), BF16)],
@@ -412,15 +411,16 @@
     for move in moves[:3]:
         move.wait()
     zl = (id_ref[0] >> 3) & 3
-    mine = shares_ref[(id_ref[0] >> 2) & 7]
+    mine = shares_ref[(id_ref[0] >> 2) & 7].astype(F32)
     upper = jnp.zeros((16, 128), F32)
     down = jnp.zeros((16, 64), F32)
     low = lax.broadcasted_iota(jnp.int32, (16, 128), 1) < 64
     for o in range(8):
         pair = jnp.where((o >> 1) == zl, 1.0, 0.0)
         quad = jnp.where((o >> 2) == (zl >> 1), 1.0, 0.0)
-        upper = upper + shares_ref[o, 0:16, :] * jnp.where(low, pair, quad)
-        down = down + shares_ref[o, 16:32, 0:64]
+        share = shares_ref[o].astype(F32)
+        upper = upper + share[0:16, :] * jnp.where(low, pair, quad)
+        down = down + share[16:32, 0:64]
     down = upper[:, 64:128] + wide_dot(down, path_ref[2], NN)
     down = upper[:, 0:64] + wide_dot(down, path_ref[1], NN)
     down = mine[16:32, 64:128] + wide_dot(down, path_ref[0], NN)
@@ -444,7 +444,7 @@
         in_specs=smem(1) + hbm(7),
         out_specs=vmem(1)[0],
         scratch_shapes=[
-            pltpu.VMEM((8, 48, 128), F32),
+            pltpu.VMEM((8, 48, 128), BF16),
             pltpu.VMEM((3, 64, 64), BF16),
             pltpu.VMEM((1, 64, 64), BF16),
             pltpu.VMEM((16, 64, 64), BF16),

time: 81.8 us -> 80.5 us (0.984)
  waiting for transfers between devices: 3.83 us -> 2.59 us
    all_to_all x1, waiting for transfers between devices: 1.58 us -> 0.59 us  [on_device(): shares = lax.all_to_all(shares, ('zl', 'core'), 0, 0, tiled=True)]
where the time goes in v4:
time: 80.5 us; the launch traced here: 79.9 us
  starting transfers between devices  41.2 us (51%)
  Pallas kernels  28.7 us (36%)
  local copies, waits for them, and re-layouts  6.54 us (8%)
  waiting for transfers between devices  2.59 us (3%)
  between operations  0.82 us (1%)
    all_to_all x1, starting transfers between devices, on_device(): lax.all_to_all(payload, ('zh', 'zl'), 0, 0, tiled=True).reshape(256, 128)  15.8 us
    pallas_call x1, Pallas kernels, near_and_prep(): pl.pallas_call(functools.partial(near_and_prep_kernel, first, last), out_...  13.2 us
    all_to_all x1, starting transfers between devices, on_device(): shares = lax.all_to_all(shares, ('zl', 'core'), 0, 0, tiled=True)  6.37 us
    all_to_all x1, starting transfers between devices, spread(): lax.all_to_all(same, axis, 0, 0, tiled=True).reshape(size * rows, 128)  5.97 us
    ppermute x1, starting transfers between devices, cyclic(): lax.ppermute(value, axis, [(i, (i + by) % size) for i in range(size)])  4.99 us
    ppermute x1, starting transfers between devices, on_device(): lax.ppermute(own, DEV, [(i, (i + 1 ^ 1) - 1) for i in range(1, 511)] + [(...  4.93 us
    pallas_call x1, Pallas kernels, near_field(): pl.pallas_call(functools.partial(near_kernel, first, last), out_shape=jax...  4.88 us
    optimization_barrier x1, local copies, waits for them, and re-layouts, on_device(): own, t1 = tie((own, t1))  4.7 us
  transfers between devices with their start and end apart: 6, of which 2 were waited for; matrix products, arithmetic and copies ran while one was open for 6% of the time, Pallas kernels for 25%

profile of v4, /device:TPU:1, one launch (start us, length us, event | category | flops | bytes accessed | tf_op | source)
XLA Modules:
  0.0 79.9 jit_solution(11058651415672974864)
XLA Ops:
  0.0 2.6 %up_pass.1 = (bf16[16,16,128]{2,1,0:T(8,128)(2,1)}, bf16[24,4096]{1,0:T(8,128)(2,1)}) custom-call(s32[1]{0:T(128)} %bitcast.id_ref, bf16[16,4096]{1,0:T(8,128)(2,1)} %rhs_hbm.1, bf16[3,4096]{1,0:T(4,128)(2,1)} %coords_hbm.1, bf16[16,64,256]{2,1,0:T(8,128)(2,1)} %basis_hbm.3, bf16[16,64,64]{2,1,0:T(8,128)(2,1)} %lt_hbm.3, bf16[1,64,64]{2,1,0:T(8,128)(2,1)} %dt_hbm.3), custom_call_target="tpu_custom_call" | custom-call | flops 20000000 | bytes 1000000 | tf_op jit(solution)/shard_map/up_pass/pallas_call | solution.py:88
  2.6 15.8 %all-to-all-start = ((bf16[16,16,128]{2,1,0:T(8,128)(2,1)}), bf16[16,16,128]{2,1,0:T(8,128)(2,1)S(1)}, u32[]{:S(2)}, u32[]{:S(2)}) async-start(bf16[16,16,128]{2,1,0:T(8,128)(2,1)} %get-tuple-element.23), calls=%async_computation | async-start | bytes 131072 | tf_op jit(solution)/shard_map/all_to_all | solution.py:479
  18.3 3.2 %collective-permute-start = (bf16[24,4096]{1,0:T(8,128)(2,1)}, bf16[24,4096]{1,0:T(8,128)(2,1)S(1)}, u32[]{:S(2)}, u32[]{:S(2)}) collective-permute-start(bf16[24,4096]{1,0:T(8,128)(2,1)} %get-tuple-element.29.own_ref), channel_id=1, source_target_pairs={{0,1},{1,0},{2,3},{3,2},{4,5},{5,4},{6,7},{7,6},{8,9},{9,8},{10,11... | collective-permute-start | bytes 589832 | tf_op jit(solution)/shard_map/ppermute | solution.py:480
  21.6 4.9 %collective-permute-start.1 = (bf16[24,4096]{1,0:T(8,128)(2,1)}, bf16[24,4096]{1,0:T(8,128)(2,1)S(1)}, u32[]{:S(2)}, u32[]{:S(2)}) collective-permute-start(bf16[24,4096]{1,0:T(8,128)(2,1)} %get-tuple-element.29.own_ref), channel_id=1, source_target_pairs={{1,2},{2,1},{3,4},{4,3},{5,6},{6,5},{7,8},{8,7},{9,10},{10,9},{11,... | collective-permute-start | bytes 589832 | tf_op jit(solution)/shard_map/ppermute | solution.py:481
  26.5 4.7 %copy.15.t1_hbm = bf16[128,64,64]{2,1,0:T(8,128)(2,1)} copy(bf16[128,64,64]{0,2,1:T(8,128)(2,1)} %param.19) | data formatting | bytes 2097152 | tf_op jit(solution)/shard_map/optimization_barrier | solution.py:482
  31.2 0.5 order_pass.1.id_ref
  31.7 0.0 collective-permute-done.swap_a_ref
  31.7 0.0 copy-start.3
  31.7 0.0 collective-permute-done.1.swap_b_ref
  31.7 0.0 copy-start.4
  31.8 0.0 all-to-all-done
  31.8 1.2 %broadcast_in_dim.2 = bf16[16,256,128]{2,1,0:T(8,128)(2,1)} broadcast(bf16[256,128]{1,0:T(8,128)(2,1)S(1)} %bitcast.7), dimensions={1,2} | broadcast | bytes 1114112 | tf_op jit(solution)/shard_map/broadcast_in_dim | solution.py:468
  32.9 6.0 %all-to-all-start.1 = ((bf16[16,256,128]{2,1,0:T(8,128)(2,1)}), bf16[16,256,128]{2,1,0:T(8,128)(2,1)S(1)}, u32[]{:S(2)}, u32[]{:S(2)}) async-start(bf16[16,256,128]{2,1,0:T(8,128)(2,1)} %broadcast_in_dim.2), calls=%async_computation.1 | async-start | bytes 2097152 | tf_op jit(solution)/shard_map/all_to_all | solution.py:469
  38.9 0.0 copy-done.3
  38.9 0.0 copy-done.4
  38.9 13.2 %near_and_prep.1 = (f32[16,3072]{1,0:T(8,128)}, bf16[98304,128]{1,0:T(8,128)(2,1)}, bf16[3,64,64]{2,1,0:T(8,128)(2,1)}) custom-call(s32[1]{0:T(128)} %order_pass.1.id_ref, s32[8,16]{1,0:T(8,128)} %bitcast.8, bf16[24,4096]{1,0:T(8,128)(2,1)} %copy-done.3, bf16[24,4096]{1,0:T(8,128)(2,1)} %get-tuple-element.29.own_ref, bf16[24,4096]{1,0:T(8,128)(2,1)} %copy-done.4, ...), custom_call_target="tpu_custom_call" | custom-call | flops 5600000000 | bytes 600000 | tf_op jit(solution)/shard_map/near_and_prep/pallas_call | solution.py:243
  52.1 2.0 %all-to-all-done.1 = bf16[16,256,128]{2,1,0:T(8,128)(2,1)S(1)} async-done(((bf16[16,256,128]{2,1,0:T(8,128)(2,1)}), bf16[16,256,128]{2,1,0:T(8,128)(2,1)S(1)}, u32[]{:S(2)}, u32[]{:S(2)}) %all-to-all-start.1) | async-done | bytes 1048608 | tf_op jit(solution)/shard_map/all_to_all | solution.py:469
  54.1 5.0 %collective-permute-start.2 = (bf16[4096,128]{1,0:T(8,128)(2,1)S(1)}, bf16[4096,128]{1,0:T(8,128)(2,1)S(1)}, u32[]{:S(2)}, u32[]{:S(2)}) collective-permute-start(bf16[4096,128]{1,0:T(8,128)(2,1)S(1)} %bitcast.4), channel_id=1, source_target_pairs={{0,4},{4,0},{1,5},{5,1},{2,6},{6,2},{3,7},{7,3},{8,12},{12,8},{9,1... | collective-permute-start | bytes 3145736 | tf_op jit(solution)/shard_map/ppermute | solution.py:463
  59.8 0.0 copy-start
  59.8 0.0 copy-start.1
  59.8 1.8 %half_pass.1 = (f32[1024,128]{1,0:T(8,128)S(1)}, bf16[10240,128]{1,0:T(8,128)(2,1)S(1)}) custom-call(bf16[4096,128]{1,0:T(8,128)(2,1)S(1)} %bitcast.5, bf16[98304,128]{1,0:T(8,128)(2,1)} %get-tuple-element.34.packed_hbm), custom_call_target="tpu_custom_call" | custom-call | flops 1000000 | bytes 5000000 | tf_op jit(solution)/shard_map/half_pass/pallas_call | solution.py:291
  61.5 0.0 collective-permute-done.2.other_ref
  61.6 0.0 copy-done
  61.6 0.0 copy-done.1
  61.6 3.1 %mid_pass.1 = bf16[8,48,128]{2,1,0:T(8,128)(2,1)} custom-call(s32[1]{0:T(128)} %bitcast.id_ref, s32[1,16]{1,0:T(1,128)S(1)} %copy-done.1, s32[1]{0:T(128)S(6)} %copy.17.fcount_ref, s32[1,4,8]{2,1,0:T(4,128)S(1)} %copy-done, bf16[4096,128]{1,0:T(8,128)(2,1)S(1)} %bitcast.6, bf16[4096,128]{1,0:T(8,128)(2,1)S(1)} %collective-permute-done.2.other_ref, ...), custom_call_target="tpu_custom_call" | custom-call | flops 300000000 | bytes 5000000 | tf_op jit(solution)/shard_map/mid_pass/pallas_call | solution.py:388
  64.6 6.4 %all-to-all-start.2 = ((bf16[8,48,128]{2,1,0:T(8,128)(2,1)}), bf16[8,48,128]{2,1,0:T(8,128)(2,1)S(1)}, u32[]{:S(2)}, u32[]{:S(2)}) async-start(bf16[8,48,128]{2,1,0:T(8,128)(2,1)} %mid_pass.1), calls=%async_computation.2 | async-start | bytes 196608 | tf_op jit(solution)/shard_map/all_to_all | solution.py:496
  71.0 4.9 %near_field.1.near_b_hbm = f32[16,1024]{1,0:T(8,128)} custom-call(s32[1]{0:T(128)} %bitcast.id_ref, s32[8,16]{1,0:T(8,128)} %bitcast.9, bf16[24,4096]{1,0:T(8,128)(2,1)} %copy-done.3, bf16[24,4096]{1,0:T(8,128)(2,1)} %get-tuple-element.29.own_ref, bf16[24,4096]{1,0:T(8,128)(2,1)} %copy-done.4), custom_call_target="tpu_custom_call" | custom-call | flops 2000000000 | bytes 600000 | tf_op jit(solution)/shard_map/near_field/pallas_call | solution.py:269
  75.9 0.6 all-to-all-done.2.shares_hbm
  76.5 0.0 copy-start.2
  76.5 0.6 copy-done.2
  77.1 2.8 %down_pass.1 = f32[16,4096]{1,0:T(8,128)} custom-call(s32[1]{0:T(128)} %bitcast.id_ref, bf16[8,48,128]{2,1,0:T(8,128)(2,1)} %copy-done.2, bf16[3,64,64]{2,1,0:T(8,128)(2,1)} %get-tuple-element.38.path_hbm, bf16[1,64,64]{2,1,0:T(8,128)(2,1)} %dt_hbm.3, bf16[16,64,64]{2,1,0:T(8,128)(2,1)} %lt_hbm.3, bf16[16,64,256]{2,1,0:T(8,128)(2,1)} %basis_hbm.3, ...), custom_call_target="tpu_custom_call" | custom-call | flops 20000000 | bytes 1500000 | tf_op jit(solution)/shard_map/down_pass/pallas_call | solution.py:441
Async XLA Ops:
  2.6 29.2 %all-to-all-start = ((bf16[16,16,128]{2,1,0:T(8,128)(2,1)}), bf16[16,16,128]{2,1,0:T(8,128)(2,1)S(1)}, u32[]{:S(2)}, u32[]{:S(2)}) async-start(bf16[16,16,128]{2,1,0:T(8,128)(2,1)} %get-tuple-element.23), calls=%async_computation | async-start | bytes 131072 | tf_op jit(solution)/shard_map/all_to_all | solution.py:479
  18.3 13.4 %collective-permute-start = (bf16[24,4096]{1,0:T(8,128)(2,1)}, bf16[24,4096]{1,0:T(8,128)(2,1)S(1)}, u32[]{:S(2)}, u32[]{:S(2)}) collective-permute-start(bf16[24,4096]{1,0:T(8,128)(2,1)} %get-tuple-element.29.own_ref), channel_id=1, source_target_pairs={{0,1},{1,0},{2,3},{3,2},{4,5},{5,4},{6,7},{7,6},{8,9},{9,8},{10,11... | collective-permute-start | bytes 589832 | tf_op jit(solution)/shard_map/ppermute | solution.py:480
  21.6 10.2 %collective-permute-start.1 = (bf16[24,4096]{1,0:T(8,128)(2,1)}, bf16[24,4096]{1,0:T(8,128)(2,1)S(1)}, u32[]{:S(2)}, u32[]{:S(2)}) collective-permute-start(bf16[24,4096]{1,0:T(8,128)(2,1)} %get-tuple-element.29.own_ref), channel_id=1, source_target_pairs={{1,2},{2,1},{3,4},{4,3},{5,6},{6,5},{7,8},{8,7},{9,10},{10,9},{11,... | collective-permute-start | bytes 589832 | tf_op jit(solution)/shard_map/ppermute | solution.py:481
  31.7 7.2 %copy-start.3 = (bf16[24,4096]{1,0:T(8,128)(2,1)}, bf16[24,4096]{1,0:T(8,128)(2,1)S(1)}, u32[]{:S(2)}) copy-start(bf16[24,4096]{1,0:T(8,128)(2,1)S(1)} %collective-permute-done.swap_a_ref) | copy-start | bytes 589828
  31.7 7.2 %copy-start.4 = (bf16[24,4096]{1,0:T(8,128)(2,1)}, bf16[24,4096]{1,0:T(8,128)(2,1)S(1)}, u32[]{:S(2)}) copy-start(bf16[24,4096]{1,0:T(8,128)(2,1)S(1)} %collective-permute-done.1.swap_b_ref) | copy-start | bytes 589828
  32.9 21.2 %all-to-all-start.1 = ((bf16[16,256,128]{2,1,0:T(8,128)(2,1)}), bf16[16,256,128]{2,1,0:T(8,128)(2,1)S(1)}, u32[]{:S(2)}, u32[]{:S(2)}) async-start(bf16[16,256,128]{2,1,0:T(8,128)(2,1)} %broadcast_in_dim.2), calls=%async_computation.1 | async-start | bytes 2097152 | tf_op jit(solution)/shard_map/all_to_all | solution.py:469
  54.1 7.4 %collective-permute-start.2 = (bf16[4096,128]{1,0:T(8,128)(2,1)S(1)}, bf16[4096,128]{1,0:T(8,128)(2,1)S(1)}, u32[]{:S(2)}, u32[]{:S(2)}) collective-permute-start(bf16[4096,128]{1,0:T(8,128)(2,1)S(1)} %bitcast.4), channel_id=1, source_target_pairs={{0,4},{4,0},{1,5},{5,1},{2,6},{6,2},{3,7},{7,3},{8,12},{12,8},{9,1... | collective-permute-start | bytes 3145736 | tf_op jit(solution)/shard_map/ppermute | solution.py:463
  59.8 1.8 %copy-start = (s32[1,4,8]{2,1,0:T(4,128)S(1)}, s32[1,4,8]{2,1,0:T(4,128)}, u32[]{:S(2)}) copy-start(s32[1,4,8]{2,1,0:T(4,128)} %tlist_ref.1) | copy-start | bytes 388
  59.8 1.8 %copy-start.1 = (s32[1,16]{1,0:T(1,128)S(1)}, s32[1,16]{1,0:T(1,128)}, u32[]{:S(2)}) copy-start(s32[1,16]{1,0:T(1,128)} %flist_ref.1) | copy-start | bytes 196
  64.6 11.8 %all-to-all-start.2 = ((bf16[8,48,128]{2,1,0:T(8,128)(2,1)}), bf16[8,48,128]{2,1,0:T(8,128)(2,1)S(1)}, u32[]{:S(2)}, u32[]{:S(2)}) async-start(bf16[8,48,128]{2,1,0:T(8,128)(2,1)} %mid_pass.1), calls=%async_computation.2 | async-start | bytes 196608 | tf_op jit(solution)/shard_map/all_to_all | solution.py:496
  76.5 0.6 copy-start.2

commit v5 on v4

--- a/solution.py
+++ b/solution.py
@@ -477,11 +477,11 @@
     tie = lax.optimization_barrier
     payload, own = up_pass(dev, rhs, coords, basis, lt, dt)
     blocks = lax.all_to_all(payload, ("zh", "zl"), 0, 0, tiled=True).reshape(256, 128)
+    swap_b = lax.ppermute(own, DEV, [(i, ((i + 1) ^ 1) - 1) for i in range(1, 511)] + [(0, 511), (511, 0)])
     swap_a = lax.ppermute(own, DEV, [(i, i ^ 1) for i in range(512)])
-    swap_b = lax.ppermute(own, DEV, [(i, ((i + 1) ^ 1) - 1) for i in range(1, 511)] + [(0, 511), (511, 0)])
     own, t1 = tie((own, t1))
     dev_a = order_pass(dev, t1)
-    blocks, swap_a, swap_b, dev_a = tie((blocks, swap_a, swap_b, dev_a))
+    blocks, swap_b, swap_a, dev_a = tie((blocks, swap_b, swap_a, dev_a))
     near_list = jnp.transpose(near_list)
     gathered = spread(blocks, ("x", "y"), 16)
     near_a, packed, path = near_and_prep(

time: 80.5 us -> 80.5 us (level)
    ppermute x1, starting transfers between devices: 3.2 us -> 1.92 us  [on_device(): swap_a = lax.ppermute(own, DEV, [(i, i ^ 1) for i in range(512)])]
where the time goes in v5:
time: 80.5 us; the launch traced here: 79.9 us
  starting transfers between devices  41.2 us (51%)
  Pallas kernels  28.7 us (36%)
  local copies, waits for them, and re-layouts  6.54 us (8%)
  waiting for transfers between devices  2.55 us (3%)
  between operations  0.82 us (1%)
    all_to_all x1, starting transfers between devices, on_device(): lax.all_to_all(payload, ('zh', 'zl'), 0, 0, tiled=True).reshape(256, 128)  15.8 us
    pallas_call x1, Pallas kernels, near_and_prep(): pl.pallas_call(functools.partial(near_and_prep_kernel, first, last), out_...  13.2 us
    all_to_all x1, starting transfers between devices, on_device(): shares = lax.all_to_all(shares, ('zl', 'core'), 0, 0, tiled=True)  6.58 us
    all_to_all x1, starting transfers between devices, spread(): lax.all_to_all(same, axis, 0, 0, tiled=True).reshape(size * rows, 128)  6.5 us
    ppermute x1, starting transfers between devices, on_device(): lax.ppermute(own, DEV, [(i, (i + 1 ^ 1) - 1) for i in range(1, 511)] + [(...  5.48 us
    ppermute x1, starting transfers between devices, cyclic(): lax.ppermute(value, axis, [(i, (i + by) % size) for i in range(size)])  5.01 us
    pallas_call x1, Pallas kernels, near_field(): pl.pallas_call(functools.partial(near_kernel, first, last), out_shape=jax...  4.89 us
    optimization_barrier x1, local copies, waits for them, and re-layouts, on_device(): own, t1 = tie((own, t1))  4.7 us
  transfers between devices with their start and end apart: 6, of which 2 were waited for; matrix products, arithmetic and copies ran while one was open for 6% of the time, Pallas kernels for 25%

profile of v5, /device:TPU:1, one launch (start us, length us, event | category | flops | bytes accessed | tf_op | source)
XLA Modules:
  0.0 79.9 jit_solution(7540088882659581625)
XLA Ops:
  0.0 2.6 %up_pass.1 = (bf16[16,16,128]{2,1,0:T(8,128)(2,1)}, bf16[24,4096]{1,0:T(8,128)(2,1)}) custom-call(s32[1]{0:T(128)} %bitcast.id_ref, bf16[16,4096]{1,0:T(8,128)(2,1)} %rhs_hbm.1, bf16[3,4096]{1,0:T(4,128)(2,1)} %coords_hbm.1, bf16[16,64,256]{2,1,0:T(8,128)(2,1)} %basis_hbm.3, bf16[16,64,64]{2,1,0:T(8,128)(2,1)} %lt_hbm.3, bf16[1,64,64]{2,1,0:T(8,128)(2,1)} %dt_hbm.3), custom_call_target="tpu_custom_call" | custom-call | flops 20000000 | bytes 1000000 | tf_op jit(solution)/shard_map/up_pass/pallas_call | solution.py:88
  2.6 15.8 %all-to-all-start = ((bf16[16,16,128]{2,1,0:T(8,128)(2,1)}), bf16[16,16,128]{2,1,0:T(8,128)(2,1)S(1)}, u32[]{:S(2)}, u32[]{:S(2)}) async-start(bf16[16,16,128]{2,1,0:T(8,128)(2,1)} %get-tuple-element.23), calls=%async_computation | async-start | bytes 131072 | tf_op jit(solution)/shard_map/all_to_all | solution.py:479
  18.3 5.5 %collective-permute-start = (bf16[24,4096]{1,0:T(8,128)(2,1)}, bf16[24,4096]{1,0:T(8,128)(2,1)S(1)}, u32[]{:S(2)}, u32[]{:S(2)}) collective-permute-start(bf16[24,4096]{1,0:T(8,128)(2,1)} %get-tuple-element.29.own_ref), channel_id=1, source_target_pairs={{1,2},{2,1},{3,4},{4,3},{5,6},{6,5},{7,8},{8,7},{9,10},{10,9},{11,... | collective-permute-start | bytes 589832 | tf_op jit(solution)/shard_map/ppermute | solution.py:480
  23.8 1.9 %collective-permute-start.1 = (bf16[24,4096]{1,0:T(8,128)(2,1)}, bf16[24,4096]{1,0:T(8,128)(2,1)S(1)}, u32[]{:S(2)}, u32[]{:S(2)}) collective-permute-start(bf16[24,4096]{1,0:T(8,128)(2,1)} %get-tuple-element.29.own_ref), channel_id=1, source_target_pairs={{0,1},{1,0},{2,3},{3,2},{4,5},{5,4},{6,7},{7,6},{8,9},{9,8},{10,11... | collective-permute-start | bytes 589832 | tf_op jit(solution)/shard_map/ppermute | solution.py:481
  25.8 4.7 %copy.15.t1_hbm = bf16[128,64,64]{2,1,0:T(8,128)(2,1)} copy(bf16[128,64,64]{0,2,1:T(8,128)(2,1)} %param.19) | data formatting | bytes 2097152 | tf_op jit(solution)/shard_map/optimization_barrier | solution.py:482
  30.5 0.5 order_pass.1.id_ref
  31.0 0.0 collective-permute-done.swap_b_ref
  31.0 0.0 copy-start.3
  31.0 0.0 collective-permute-done.1.swap_a_ref
  31.0 0.0 copy-start.4
  31.0 0.0 all-to-all-done
  31.0 1.2 %broadcast_in_dim.2 = bf16[16,256,128]{2,1,0:T(8,128)(2,1)} broadcast(bf16[256,128]{1,0:T(8,128)(2,1)S(1)} %bitcast.7), dimensions={1,2} | broadcast | bytes 1114112 | tf_op jit(solution)/shard_map/broadcast_in_dim | solution.py:468
  32.2 6.5 %all-to-all-start.1 = ((bf16[16,256,128]{2,1,0:T(8,128)(2,1)}), bf16[16,256,128]{2,1,0:T(8,128)(2,1)S(1)}, u32[]{:S(2)}, u32[]{:S(2)}) async-start(bf16[16,256,128]{2,1,0:T(8,128)(2,1)} %broadcast_in_dim.2), calls=%async_computation.1 | async-start | bytes 2097152 | tf_op jit(solution)/shard_map/all_to_all | solution.py:469
  38.7 0.0 copy-done.3
  38.7 0.0 copy-done.4
  38.7 13.2 %near_and_prep.1 = (f32[16,3072]{1,0:T(8,128)}, bf16[98304,128]{1,0:T(8,128)(2,1)}, bf16[3,64,64]{2,1,0:T(8,128)(2,1)}) custom-call(s32[1]{0:T(128)} %order_pass.1.id_ref, s32[8,16]{1,0:T(8,128)} %bitcast.8, bf16[24,4096]{1,0:T(8,128)(2,1)} %copy-done.4, bf16[24,4096]{1,0:T(8,128)(2,1)} %get-tuple-element.29.own_ref, bf16[24,4096]{1,0:T(8,128)(2,1)} %copy-done.3, ...), custom_call_target="tpu_custom_call" | custom-call | flops 5600000000 | bytes 600000 | tf_op jit(solution)/shard_map/near_and_prep/pallas_call | solution.py:243
  51.9 2.0 %all-to-all-done.1 = bf16[16,256,128]{2,1,0:T(8,128)(2,1)S(1)} async-done(((bf16[16,256,128]{2,1,0:T(8,128)(2,1)}), bf16[16,256,128]{2,1,0:T(8,128)(2,1)S(1)}, u32[]{:S(2)}, u32[]{:S(2)}) %all-to-all-start.1) | async-done | bytes 1048608 | tf_op jit(solution)/shard_map/all_to_all | solution.py:469
  53.9 5.0 %collective-permute-start.2 = (bf16[4096,128]{1,0:T(8,128)(2,1)S(1)}, bf16[4096,128]{1,0:T(8,128)(2,1)S(1)}, u32[]{:S(2)}, u32[]{:S(2)}) collective-permute-start(bf16[4096,128]{1,0:T(8,128)(2,1)S(1)} %bitcast.4), channel_id=1, source_target_pairs={{0,4},{4,0},{1,5},{5,1},{2,6},{6,2},{3,7},{7,3},{8,12},{12,8},{9,1... | collective-permute-start | bytes 3145736 | tf_op jit(solution)/shard_map/ppermute | solution.py:463
  59.5 0.0 copy-start
  59.5 0.0 copy-start.1
  59.5 1.8 %half_pass.1 = (f32[1024,128]{1,0:T(8,128)S(1)}, bf16[10240,128]{1,0:T(8,128)(2,1)S(1)}) custom-call(bf16[4096,128]{1,0:T(8,128)(2,1)S(1)} %bitcast.5, bf16[98304,128]{1,0:T(8,128)(2,1)} %get-tuple-element.34.packed_hbm), custom_call_target="tpu_custom_call" | custom-call | flops 1000000 | bytes 5000000 | tf_op jit(solution)/shard_map/half_pass/pallas_call | solution.py:291
  61.3 0.0 collective-permute-done.2.other_ref
  61.3 0.0 copy-done
  61.3 0.0 copy-done.1
  61.3 3.1 %mid_pass.1 = bf16[8,48,128]{2,1,0:T(8,128)(2,1)} custom-call(s32[1]{0:T(128)} %bitcast.id_ref, s32[1,16]{1,0:T(1,128)S(1)} %copy-done.1, s32[1]{0:T(128)S(6)} %copy.17.fcount_ref, s32[1,4,8]{2,1,0:T(4,128)S(1)} %copy-done, bf16[4096,128]{1,0:T(8,128)(2,1)S(1)} %bitcast.6, bf16[4096,128]{1,0:T(8,128)(2,1)S(1)} %collective-permute-done.2.other_ref, ...), custom_call_target="tpu_custom_call" | custom-call | flops 300000000 | bytes 5000000 | tf_op jit(solution)/shard_map/mid_pass/pallas_call | solution.py:388
  64.4 6.6 %all-to-all-start.2 = ((bf16[8,48,128]{2,1,0:T(8,128)(2,1)}), bf16[8,48,128]{2,1,0:T(8,128)(2,1)S(1)}, u32[]{:S(2)}, u32[]{:S(2)}) async-start(bf16[8,48,128]{2,1,0:T(8,128)(2,1)} %mid_pass.1), calls=%async_computation.2 | async-start | bytes 196608 | tf_op jit(solution)/shard_map/all_to_all | solution.py:496
  71.0 4.9 %near_field.1.near_b_hbm = f32[16,1024]{1,0:T(8,128)} custom-call(s32[1]{0:T(128)} %bitcast.id_ref, s32[8,16]{1,0:T(8,128)} %bitcast.9, bf16[24,4096]{1,0:T(8,128)(2,1)} %copy-done.4, bf16[24,4096]{1,0:T(8,128)(2,1)} %get-tuple-element.29.own_ref, bf16[24,4096]{1,0:T(8,128)(2,1)} %copy-done.3), custom_call_target="tpu_custom_call" | custom-call | flops 2000000000 | bytes 600000 | tf_op jit(solution)/shard_map/near_field/pallas_call | solution.py:269
  75.9 0.6 all-to-all-done.2.shares_hbm
  76.5 0.0 copy-start.2
  76.5 0.6 copy-done.2
  77.1 2.8 %down_pass.1 = f32[16,4096]{1,0:T(8,128)} custom-call(s32[1]{0:T(128)} %bitcast.id_ref, bf16[8,48,128]{2,1,0:T(8,128)(2,1)} %copy-done.2, bf16[3,64,64]{2,1,0:T(8,128)(2,1)} %get-tuple-element.38.path_hbm, bf16[1,64,64]{2,1,0:T(8,128)(2,1)} %dt_hbm.3, bf16[16,64,64]{2,1,0:T(8,128)(2,1)} %lt_hbm.3, bf16[16,64,256]{2,1,0:T(8,128)(2,1)} %basis_hbm.3, ...), custom_call_target="tpu_custom_call" | custom-call | flops 20000000 | bytes 1500000 | tf_op jit(solution)/shard_map/down_pass/pallas_call | solution.py:441
Async XLA Ops:
  2.6 28.5 %all-to-all-start = ((bf16[16,16,128]{2,1,0:T(8,128)(2,1)}), bf16[16,16,128]{2,1,0:T(8,128)(2,1)S(1)}, u32[]{:S(2)}, u32[]{:S(2)}) async-start(bf16[16,16,128]{2,1,0:T(8,128)(2,1)} %get-tuple-element.23), calls=%async_computation | async-start | bytes 131072 | tf_op jit(solution)/shard_map/all_to_all | solution.py:479
  18.3 12.7 %collective-permute-start = (bf16[24,4096]{1,0:T(8,128)(2,1)}, bf16[24,4096]{1,0:T(8,128)(2,1)S(1)}, u32[]{:S(2)}, u32[]{:S(2)}) collective-permute-start(bf16[24,4096]{1,0:T(8,128)(2,1)} %get-tuple-element.29.own_ref), channel_id=1, source_target_pairs={{1,2},{2,1},{3,4},{4,3},{5,6},{6,5},{7,8},{8,7},{9,10},{10,9},{11,... | collective-permute-start | bytes 589832 | tf_op jit(solution)/shard_map/ppermute | solution.py:480
  23.8 7.2 %collective-permute-start.1 = (bf16[24,4096]{1,0:T(8,128)(2,1)}, bf16[24,4096]{1,0:T(8,128)(2,1)S(1)}, u32[]{:S(2)}, u32[]{:S(2)}) collective-permute-start(bf16[24,4096]{1,0:T(8,128)(2,1)} %get-tuple-element.29.own_ref), channel_id=1, source_target_pairs={{0,1},{1,0},{2,3},{3,2},{4,5},{5,4},{6,7},{7,6},{8,9},{9,8},{10,11... | collective-permute-start | bytes 589832 | tf_op jit(solution)/shard_map/ppermute | solution.py:481
  31.0 7.7 %copy-start.3 = (bf16[24,4096]{1,0:T(8,128)(2,1)}, bf16[24,4096]{1,0:T(8,128)(2,1)S(1)}, u32[]{:S(2)}) copy-start(bf16[24,4096]{1,0:T(8,128)(2,1)S(1)} %collective-permute-done.swap_b_ref) | copy-start | bytes 589828
  31.0 7.7 %copy-start.4 = (bf16[24,4096]{1,0:T(8,128)(2,1)}, bf16[24,4096]{1,0:T(8,128)(2,1)S(1)}, u32[]{:S(2)}) copy-start(bf16[24,4096]{1,0:T(8,128)(2,1)S(1)} %collective-permute-done.1.swap_a_ref) | copy-start | bytes 589828
  32.2 21.6 %all-to-all-start.1 = ((bf16[16,256,128]{2,1,0:T(8,128)(2,1)}), bf16[16,256,128]{2,1,0:T(8,128)(2,1)S(1)}, u32[]{:S(2)}, u32[]{:S(2)}) async-start(bf16[16,256,128]{2,1,0:T(8,128)(2,1)} %broadcast_in_dim.2), calls=%async_computation.1 | async-start | bytes 2097152 | tf_op jit(solution)/shard_map/all_to_all | solution.py:469
  53.9 7.5 %collective-permute-start.2 = (bf16[4096,128]{1,0:T(8,128)(2,1)S(1)}, bf16[4096,128]{1,0:T(8,128)(2,1)S(1)}, u32[]{:S(2)}, u32[]{:S(2)}) collective-permute-start(bf16[4096,128]{1,0:T(8,128)(2,1)S(1)} %bitcast.4), channel_id=1, source_target_pairs={{0,4},{4,0},{1,5},{5,1},{2,6},{6,2},{3,7},{7,3},{8,12},{12,8},{9,1... | collective-permute-start | bytes 3145736 | tf_op jit(solution)/shard_map/ppermute | solution.py:463
  59.5 1.8 %copy-start = (s32[1,4,8]{2,1,0:T(4,128)S(1)}, s32[1,4,8]{2,1,0:T(4,128)}, u32[]{:S(2)}) copy-start(s32[1,4,8]{2,1,0:T(4,128)} %tlist_ref.1) | copy-start | bytes 388
  59.5 1.8 %copy-start.1 = (s32[1,16]{1,0:T(1,128)S(1)}, s32[1,16]{1,0:T(1,128)}, u32[]{:S(2)}) copy-start(s32[1,16]{1,0:T(1,128)} %flist_ref.1) | copy-start | bytes 196
  64.4 12.1 %all-to-all-start.2 = ((bf16[8,48,128]{2,1,0:T(8,128)(2,1)}), bf16[8,48,128]{2,1,0:T(8,128)(2,1)S(1)}, u32[]{:S(2)}, u32[]{:S(2)}) async-start(bf16[8,48,128]{2,1,0:T(8,128)(2,1)} %mid_pass.1), calls=%async_computation.2 | async-start | bytes 196608 | tf_op jit(solution)/shard_map/all_to_all | solution.py:496
  76.5 0.6 copy-start.2
